TPU v7x, 32 devices: a whole 2x2x4 slice. The times are simulated.
32 devices in a mesh: qx: 4 (over y, core), qy: 8 (over z, x).
Axes of the slice: x: 2, y: 2, z: 4, core: 2. Of those that a mesh axis runs over, the one named last changes fastest.
Arguments:
- positions: float32 [16, 32, 2, 256], replicated, may hold values from 0 to 32, as said below
- samples: bfloat16 [16, 32, 256, 256], P('qx', 'qy'), may hold values from -6 to 6
- leaf_basis: bfloat16 [16, 32, 256, 256], P('qx', 'qy'), may hold values from -0.375 to 0.375
- transfer_one: bfloat16 [16, 32, 256, 256], P('qx', 'qy'), may hold values from -0.25 to 0.25
- transfer_two: bfloat16 [8, 16, 256, 256], P('qx', 'qy'), may hold values from -0.25 to 0.25
- couplings: bfloat16 [3, 20, 256, 256], replicated, may hold values from -0.078125 to 0.078125
- near_lists: int32 [16, 32, 9], P('qx', 'qy'), may hold values from -1 to 511, as said below
- far_zero: int32 [16, 32, 27], P('qx', 'qy'), may hold values from -1 to 511, as said below
- far_one: int32 [8, 16, 27], P('qx', 'qy'), may hold values from -1 to 127, as said below
- far_two: int32 [4, 8, 27], P('qx', 'qy'), may hold values from -1 to 31, as said below
Outputs:
- product: bfloat16 [16, 32, 256, 256], P('qx', 'qy')
Inputs may be any that keep to these rules, and one draw needn't show every extreme that they name: Site p of leaf (i, j) lies at positions[i, j, 0, p] between i and i + 1 and positions[i, j, 1, p] between j and j + 1. `near_lists`: every entry of the list of leaf (i, j) is -1 or the id r * 32 + c of a leaf (r, c) with abs(r - i) <= 1 and abs(c - j) <= 1; the leaf's own id is always in its list, and no id stands twice. `far_zero`: every entry of the list of leaf (i, j) is -1 or the id r * 32 + c of a leaf (r, c) with max(abs(r - i), abs(c - j)) >= 2 whose parent (r // 2, c // 2) is within one step of (i // 2, j // 2) along each coordinate; no id stands twice. `far_one`: every entry of the list of level-1 cell (i, j) is -1 or the id r * 16 + c of a level-1 cell (r, c) with max(abs(r - i), abs(c - j)) >= 2 and (r // 2, c // 2) within one step of (i // 2, j // 2) along each coordinate; no id stands twice. `far_two`: every entry of the list of level-2 cell (i, j) is -1 or the id r * 8 + c of a level-2 cell (r, c) with max(abs(r - i), abs(c - j)) >= 2 and (r // 2, c // 2) within one step of (i // 2, j // 2) along each coordinate; no id stands twice.
All inputs are finite; a program needn't handle non-finite values.
Results may differ from a plain program's by a relative error of at most 0.0085.
Values may be sent and summed in bfloat16 or wider, within the bound.
No kernel may reach another device: no remote copies, remote signals or barrier semaphores. Data moves between devices by JAX's collectives and lax.ppermute only.
A program may use at most 256 MiB of HBM per device.

v0:
```python
import functools

import jax
import jax.numpy as jnp
import numpy as np
from jax import lax
from jax.experimental import pallas as pl
from jax.experimental.pallas import tpu as pltpu
from jax.sharding import PartitionSpec as P

root_three = 1.7320508075688772
length_scale = 1.0
VMEM = pltpu.VMEM
SMEM = pltpu.SMEM
F32 = jnp.float32
BF16 = jnp.bfloat16
BIG = 64 * 1024 * 1024 - 256 * 1024


def nn(a, b):
    return lax.dot_general(a, b, (((1,), (0,)), ((), ())), preferred_element_type=F32)


def nt(a, b):
    return lax.dot_general(a, b, (((1,), (1,)), ((), ())), preferred_element_type=F32)


def tn(a, b):
    return lax.dot_general(a, b, (((0,), (0,)), ((), ())), preferred_element_type=F32)


def params():
    return pltpu.CompilerParams(vmem_limit_bytes=BIG)


def cost(products, bytes_accessed):
    return pl.CostEstimate(
        flops=products * 2 * 256**3 // 8, bytes_accessed=bytes_accessed // 8, transcendentals=0
    )


def half_offsets():
    kept = []
    for u in range(-3, 4):
        for v in range(-3, 4):
            if max(abs(u), abs(v)) >= 2 and (u > 0 or (u == 0 and v > 0)):
                kept.append((u, v))
    return kept


HALF_OFFSETS = half_offsets()


def class_plan(a, b):
    plain, turned = [], []
    for w in range(36):
        u, v = w // 6 - 2 - a, w % 6 - 2 - b
        if max(abs(u), abs(v)) < 2:
            continue
        if (u, v) in HALF_OFFSETS:
            plain.append((w, HALF_OFFSETS.index((u, v))))
        else:
            turned.append((w, HALF_OFFSETS.index((-u, -v))))
    return plain, turned


LOG2E = 1.4426950408889634
TILE_SCALE = 256 ** -0.5


def tiles(n, dtype=BF16):
    return jax.ShapeDtypeStruct((n, 256, 256), dtype)


ANY_SPEC = pl.BlockSpec(memory_space=pltpu.HBM)
SMEM_SPEC = pl.BlockSpec(memory_space=SMEM)
VMEM_SPEC = pl.BlockSpec(memory_space=VMEM)


class Copies:
    def __init__(self, sems):
        self.sems = sems
        self.started = []

    def start(self, src, dst):
        copy = pltpu.make_async_copy(src, dst, self.sems.at[len(self.started)])
        copy.start()
        self.started.append(copy)
        return copy

    def wait(self):
        for copy in self.started:
            copy.wait()


def coef_kernel(
    samples, basis, t_one, t_two, up, down, left, right, upper, cell,
    sv, bv, t1v, t2v, cv, uv, in_sems, out_sems,
):
    into = Copies(in_sems)
    out = Copies(out_sems)
    rows = []
    for x in range(4):
        rows.append(
            (
                into.start(samples.at[x], sv.at[x]),
                into.start(basis.at[x], bv.at[x]),
                into.start(t_one.at[x], t1v.at[x]),
            )
        )
    last = into.start(t_two, t2v)
    for x in range(4):
        rows[x][0].wait()
        rows[x][1].wait()
        for y in range(4):
            cv[x * 4 + y] = tn(sv[x, y], bv[x, y]).astype(BF16)
        own = cv.at[4 * x : 4 * x + 4]
        out.start(own, (up if x < 2 else down).at[4 * (x % 2) : 4 * (x % 2) + 4])
        out.start(cv.at[4 * x : 4 * x + 2], left.at[2 * x : 2 * x + 2])
        out.start(cv.at[4 * x + 2 : 4 * x + 4], right.at[2 * x : 2 * x + 2])
        out.start(sv.at[x, 0], left.at[8 + x])
        out.start(sv.at[x, 3], right.at[8 + x])
        if x == 0:
            out.start(sv.at[x], up.at[8:12])
        if x == 3:
            out.start(sv.at[x], down.at[8:12])
        if x % 2 == 1:
            rows[x - 1][2].wait()
            rows[x][2].wait()
            for y in range(2):
                kids = [(x - 1 + a, 2 * y + b) for a in range(2) for b in range(2)]
                lhs = jnp.concatenate([cv[k * 4 + m] for k, m in kids], axis=1)
                rhs = jnp.concatenate([t1v[k] for k in kids], axis=0)
                uv[x // 2 * 2 + y] = nn(lhs, rhs).astype(BF16)
    last.wait()
    lhs = jnp.concatenate([uv[k] for k in range(4)], axis=1)
    rhs = jnp.concatenate([t2v[k // 2, k % 2] for k in range(4)], axis=0)
    uv[4] = nn(lhs, rhs).astype(BF16)
    out.start(uv, upper)
    out.start(uv.at[4:5], cell)
    out.wait()


def coefficients(samples, basis, t_one, t_two):
    return pl.pallas_call(
        coef_kernel,
        out_shape=[tiles(n) for n in (12, 12, 12, 12, 5, 1)],
        in_specs=[ANY_SPEC] * 4,
        out_specs=[ANY_SPEC] * 6,
        scratch_shapes=[
            VMEM((4, 4, 256, 256), BF16),
            VMEM((4, 4, 256, 256), BF16),
            VMEM((4, 4, 256, 256), BF16),
            VMEM((2, 2, 256, 256), BF16),
            VMEM((16, 256, 256), BF16),
            VMEM((5, 256, 256), BF16),
            pltpu.SemaphoreType.DMA((13,)),
            pltpu.SemaphoreType.DMA((24,)),
        ],
        compiler_params=params(),
        cost_estimate=cost(170, 12 << 20),
        name="coefficients",
    )(samples, basis, t_one, t_two)


def assembled(name, sources, pieces, ranges, stated=35):
    count = sum(n for _, _, n in pieces)

    def kernel(*refs):
        ins, outs = refs[: len(sources)], refs[len(sources) : -3]
        held, in_sems, out_sems = refs[-3:]
        into = Copies(in_sems)
        at = 0
        for source, first, n in pieces:
            into.start(ins[source].at[first : first + n], held.at[at : at + n])
            at += n
        into.wait()
        out = Copies(out_sems)
        for (first, last), ref in zip(ranges, outs):
            out.start(held.at[first:last], ref)
        out.wait()

    return pl.pallas_call(
        kernel,
        out_shape=[tiles(last - first) for first, last in ranges],
        in_specs=[ANY_SPEC] * len(sources),
        out_specs=[ANY_SPEC] * len(ranges),
        scratch_shapes=[
            VMEM((count, 256, 256), BF16),
            pltpu.SemaphoreType.DMA((len(pieces),)),
            pltpu.SemaphoreType.DMA((len(ranges),)),
        ],
        compiler_params=params(),
        cost_estimate=cost(stated, 0),
        name=name,
    )(*sources)


def halo_places():
    numbers = {}
    for r in range(4):
        for c in range(4):
            for k in range(9):
                y, x = r + k // 3 - 1, c + k % 3 - 1
                if not (0 <= y < 4 and 0 <= x < 4):
                    numbers[r * 4 + c, k] = len(numbers)
    return numbers


HALO = halo_places()
N_HALO = len(HALO) // 2


def split3(x):
    first = x.astype(BF16).astype(F32)
    rest = x - first
    second = rest.astype(BF16).astype(F32)
    return first, second, rest - second


def site_features(x, y):
    n = lax.broadcasted_iota(jnp.int32, (8, 256), 0)
    square = x * x + y * y
    target, source = [], []
    for parts in (split3(x), split3(y)):
        first, second, third = parts
        target.append(jnp.where(n < 3, first, jnp.where(n < 5, second, jnp.where(n < 6, third, 0.0))))
        other = jnp.where(
            (n == 0) | (n == 3) | (n == 5),
            first,
            jnp.where((n == 1) | (n == 4), second, jnp.where(n == 2, third, 0.0)),
        )
        source.append(-2.0 * other)
    first, second, third = split3(square)
    low = jnp.where(n == 0, first, jnp.where(n == 1, second, third))
    high = jnp.where(n == 3, first, jnp.where(n == 4, second, third))
    one = jnp.where(n < 6, 1.0, 0.0)
    target.append(jnp.where(n < 3, low, one))
    source.append(jnp.where(n < 3, 1.0, jnp.where(n < 6, high, 0.0)))
    zero = jnp.zeros((8, 256), F32)
    return jnp.concatenate(target + [zero], axis=0), jnp.concatenate(source + [zero], axis=0)


def near_kernel(
    first, with_far, grid_rows, grid_cols, lists, far_zero, positions, own, *rest
):
    if with_far:
        flags, couplings, up, down, above, below, near_out, halo_out, field_out = rest[:9]
        table, far_held, field, far_sems, field_sems = rest[9:14]
        rest = rest[14:]
    else:
        near_out, halo_out, flags = rest[:3]
        rest = rest[3:]
    held, target_feat, source_feat, halo, made, near, floors, sems, halo_sems, near_sems = rest
    copy = pltpu.make_async_copy(own, held, sems.at[0])
    copy.start()
    out = Copies(halo_sems)
    sums_out = Copies(near_sems)
    if with_far:
        far_in = Copies(far_sems)
        far_in.start(couplings.at[0], table)
        for n, src in enumerate((above, up, down, below)):
            far_in.start(src.at[0:8], far_held.at[8 * n : 8 * n + 8])
        far_held[32] = jnp.zeros((256, 256), BF16)
        field_copies = Copies(field_sems)
    first_row = lax.axis_index("qx") * 4
    first_col = lax.axis_index("qy") * 4
    scale = root_three / length_scale
    mid_row = first_row.astype(F32) + 2.0
    mid_col = first_col.astype(F32) + 2.0
    first_place = first // 4 * 6

    def features(n, carry):
        r = jnp.clip(first_row + (first_place + n) // 6 - 1, 0, grid_rows - 1)
        c = jnp.clip(first_col + n % 6 - 1, 0, grid_cols - 1)
        here = positions[r * grid_cols + c]
        target, source = site_features(
            (here[0:1] - mid_row) * scale, (here[1:2] - mid_col) * scale
        )
        target_feat[n] = target
        source_feat[n] = source.astype(BF16)
        return carry

    lax.fori_loop(0, 24, features, 0)

    def mark(t):
        r, c = t // 4, t % 4
        mark_listed(
            lambda e: far_zero[r, c, e],
            flags,
            t,
            first_row + r // 2 * 2 - 2,
            first_col + c // 2 * 2 - 2,
            grid_cols,
        )

    def make(m):
        t = first + m
        r, c = t // 4, t % 4
        slot = m % 2 * 9
        for k in range(9):
            floors[m * 10 + k] = 1e6
        for e in range(9):
            entry = lists[r, c, e]
            source_row = jnp.maximum(entry, 0) // grid_cols
            source_col = jnp.maximum(entry, 0) - source_row * grid_cols
            k = (source_row - first_row - r + 1) * 3 + source_col - first_col - c + 1
            floors[m * 10 + jnp.where(entry >= 0, k, 9)] = 1e-24
        if not with_far:
            mark(2 * m)
            mark(2 * m + 1)
        place = (m // 4 + 1) * 6 + c + 1
        target = target_feat[place].T.astype(BF16)
        for k in range(9):
            square = nn(target, source_feat[place + (k // 3 - 1) * 6 + k % 3 - 1])
            square = jnp.maximum(square, floors[m * 10 + k])
            far = square * lax.rsqrt(square)
            tile = ((far + 1.0) * jnp.exp2(far * -LOG2E)).astype(BF16)
            if (t, k) in HALO:
                number = HALO[t, k] % N_HALO
                halo[number] = tile
                out.start(halo.at[number], halo_out.at[number])
            else:
                made[slot + k] = tile

    def use(m):
        t = first + m
        slot = m % 2 * 9
        found = [k for k in range(9) if (t, k) not in HALO]
        lhs = jnp.concatenate([made[slot + k] for k in found], axis=1)
        blocks = [held[t + (k // 3 - 1) * 4 + k % 3 - 1] for k in found]
        near[m] = nn(lhs, jnp.concatenate(blocks, axis=0))
        sums_out.start(near.at[m], near_out.at[m])

    make(0)
    copy.wait()
    if with_far:
        far_in.wait()
    for m in range(1, 8):
        make(m)
        if with_far and m % 2 == 1:
            a, b = m // 4, m // 2 % 2
            sums = level_zero_sums("inner", a, b, flags, table, far_held, 32)
            for p in PARENTS:
                t = number_of(a, b, p)
                field[t] = sums[p]
                field_copies.start(field.at[t], field_out.at[t])
        use(m - 1)
    use(7)
    out.wait()
    sums_out.wait()
    if with_far:
        field_copies.wait()


def near_call(first, grid_rows, grid_cols, lists, far_zero, positions, own, far=()):
    out_shape = [tiles(8, F32), tiles(N_HALO)]
    out_specs = [ANY_SPEC, ANY_SPEC]
    scratch = []
    if far:
        out_shape.append(tiles(16, F32))
        out_specs.append(ANY_SPEC)
        scratch = [
            VMEM((20, 256, 256), BF16),
            VMEM((33, 256, 256), BF16),
            VMEM((16, 256, 256), F32),
            pltpu.SemaphoreType.DMA((5,)),
            pltpu.SemaphoreType.DMA((16,)),
        ]
    else:
        out_shape.append(jax.ShapeDtypeStruct((16, 37), jnp.int32))
        out_specs.append(SMEM_SPEC)
    return pl.pallas_call(
        functools.partial(near_kernel, first, bool(far), grid_rows, grid_cols),
        out_shape=out_shape,
        in_specs=[SMEM_SPEC, SMEM_SPEC, VMEM_SPEC, ANY_SPEC]
        + ([SMEM_SPEC] + [ANY_SPEC] * 5 if far else []),
        out_specs=out_specs,
        scratch_shapes=scratch
        + [
            VMEM((16, 256, 256), BF16),
            VMEM((24, 32, 256), F32),
            VMEM((24, 32, 256), BF16),
            VMEM((N_HALO, 256, 256), BF16),
            VMEM((18, 256, 256), BF16),
            VMEM((8, 256, 256), F32),
            pltpu.SMEM((80,), F32),
            pltpu.SemaphoreType.DMA((1,)),
            pltpu.SemaphoreType.DMA((N_HALO,)),
            pltpu.SemaphoreType.DMA((8,)),
        ],
        compiler_params=params(),
        cost_estimate=cost(600 if far else 12000, 8 << 20),
        name="near_and_inner_far" if far else "near_first",
    )(lists, far_zero, positions, own, *far)


def mark_listed(entries, flags, n, first_row, first_col, grid_cols):
    for w in range(36):
        flags[n, w] = 0
    for e in range(27):
        entry = entries(e)
        row = jnp.maximum(entry, 0) // grid_cols
        col = jnp.maximum(entry, 0) - row * grid_cols
        w = (row - first_row) * 6 + col - first_col
        flags[n, jnp.where(entry >= 0, jnp.clip(w, 0, 35), 36)] = 1


def dot_group(held, couplings, turned, group):
    rows = len(group[0][1])
    lhs = [
        jnp.concatenate([held[places[n]] for _, places in group], axis=1) for n in range(rows)
    ]
    lhs = jnp.concatenate(lhs, axis=0) if rows > 1 else lhs[0]
    if turned:
        return nn(lhs, jnp.concatenate([couplings[k] for k, _ in group], axis=0))
    return nt(lhs, jnp.concatenate([couplings[k] for k, _ in group], axis=1))


def coupled(plan, couplings, held, places):
    total = None
    for turned in (0, 1):
        group = [(k, [places(w)]) for w, k in plan[turned]]
        part = dot_group(held, couplings, turned, group)
        total = part if total is None else total + part
    return total


def upper_kernel(
    grid_cols, n_rows, far_one, far_two, couplings, t_two, row, row_e, row_d, cells, cells_e, down,
    held_one, held_two, field_two, flags, sems,
):
    n_two = 6 * n_rows
    zero_one, zero_two = 36, 2 * n_two
    copies = Copies(sems)
    copies.start(cells, held_two.at[0:n_two])
    copies.start(cells_e, held_two.at[n_two : 2 * n_two])
    copies.start(row, held_one.at[0:12])
    copies.start(row_e, held_one.at[12:24])
    copies.start(row_d, held_one.at[24:36])
    held_one[zero_one] = jnp.zeros((256, 256), BF16)
    held_two[zero_two] = jnp.zeros((256, 256), BF16)
    i = lax.axis_index("qx")
    j = lax.axis_index("qy")
    a = i % 2
    b = j % 2
    for t in range(4):
        mark_listed(
            lambda e: far_one[t // 2, t % 2, e], flags, t, 2 * i - 2, 2 * j - 2, 2 * grid_cols
        )
    mark_listed(
        lambda e: far_two[0, 0, e], flags, 4, i // 2 * 2 - 2, j // 2 * 2 - 2, grid_cols
    )
    core_at = [jnp.where(a == 0, 0, n_two), jnp.where(a == 0, n_two, 0)]
    y_at = [2, 0, 2] if n_rows == 2 else [2, 0, 4]
    pair_tiles = 2 * n_rows
    z_at = [
        jnp.where(b == 0, pair_tiles, 2 * pair_tiles),
        0,
        jnp.where(b == 0, 2 * pair_tiles, pair_tiles),
    ]
    x_at = [b, 1 - b]

    def place_two(w):
        r, c = w // 6, w % 6
        place = core_at[r % 2] + y_at[r // 2] + z_at[c // 2] + x_at[c % 2]
        return jnp.where(flags[4, w] == 1, place, zero_two)

    row_at = [jnp.where(a == 0, 24, 12), 0, jnp.where(a == 0, 12, 24)]
    col_at = [jnp.where(b == 0, 8, 4), 0, jnp.where(b == 0, 4, 8)]

    def place_one(t, w):
        r, c = w // 6, w % 6
        place = row_at[r // 2] + col_at[c // 2] + (r % 2) * 2 + c % 2
        return jnp.where(flags[t, w] == 1, place, zero_one)

    for copy in copies.started[:2]:
        copy.wait()
    for u in range(2):
        for v in range(2):

            @pl.when((a == u) & (b == v))
            def _():
                field_two[...] = coupled(
                    class_plan(u, v), couplings.at[1], held_two, place_two
                ).astype(BF16)

    for copy in copies.started[2:]:
        copy.wait()
    for u in range(2):
        for v in range(2):
            t = u * 2 + v
            field = coupled(
                class_plan(u, v), couplings.at[0], held_one, functools.partial(place_one, t)
            )
            down[t] = (field + nt(field_two[...], t_two[u, v])).astype(BF16)


def upper_levels(grid_cols, far_one, far_two, couplings, t_two, row, row_e, row_d, cells, cells_e):
    n_two = cells.shape[0]
    return pl.pallas_call(
        functools.partial(upper_kernel, grid_cols, n_two // 6),
        grid=(1,),
        out_shape=tiles(4),
        in_specs=[
            SMEM_SPEC,
            SMEM_SPEC,
            pl.BlockSpec(
                (pl.Element(2), pl.Element(20), pl.Element(256), pl.Element(256)),
                lambda g: (1, 0, 0, 0),
            ),
            pl.BlockSpec((2, 2, 256, 256), lambda g: (0, 0, 0, 0)),
        ]
        + [ANY_SPEC] * 5,
        out_specs=pl.BlockSpec((4, 256, 256), lambda g: (0, 0, 0)),
        scratch_shapes=[
            VMEM((37, 256, 256), BF16),
            VMEM((2 * n_two + 1, 256, 256), BF16),
            VMEM((256, 256), BF16),
            pltpu.SMEM((5, 37), jnp.int32),
            pltpu.SemaphoreType.DMA((5,)),
        ],
        compiler_params=params(),
        cost_estimate=cost(340, 14 << 20),
        name="upper_levels",
    )(far_one, far_two, couplings, t_two, row, row_e, row_d, cells, cells_e)


def source_of(x, y, w):
    r, c = 2 * x + w // 6, 2 * y + w % 6
    if 2 <= c < 6:
        return "inner", r * 4 + c - 2
    side = 0 if c < 2 else 1
    c = c if c < 2 else c - 6
    if 2 <= r < 6:
        return "sides", side * 8 + (r - 2) * 2 + c
    return "corners", (0 if r < 2 else 8) + side * 4 + (r if r < 2 else r - 6) * 2 + c


PARENTS = [(x, y) for x in range(2) for y in range(2)]


def number_of(a, b, parent):
    x, y = parent
    return (2 * x + a) * 4 + 2 * y + b


def level_zero_sums(kind, a, b, flags, couplings, held, zero):
    plan = class_plan(a, b)
    sums = {}
    for turned in (0, 1):
        groups = {}
        for w, k in plan[turned]:
            members = tuple(p for p in PARENTS if source_of(*p, w)[0] == kind)
            if members:
                groups.setdefault(members, []).append((w, k))
        for members, entries in groups.items():
            group = []
            for w, k in entries:
                places = [
                    jnp.where(flags[number_of(a, b, p), w] == 1, source_of(*p, w)[1], zero)
                    for p in members
                ]
                group.append((k, places))
            total = dot_group(held, couplings, turned, group)
            for n, p in enumerate(members):
                part = total[256 * n : 256 * n + 256]
                sums[p] = part if p not in sums else sums[p] + part
    return sums


def grouped(x):
    return x.reshape(2, 2, 2, 2, 256, 256)


CLASS_BLOCK = pl.BlockSpec((2, 1, 2, 1, 256, 256), lambda g: (0, g // 2, 0, g % 2, 0, 0))
COUPLING_BLOCK = pl.BlockSpec((1, 20, 256, 256), lambda g: (0, 0, 0, 0))
GROUPED_F32 = jax.ShapeDtypeStruct((2, 2, 2, 2, 256, 256), F32)


def each_class(step, body):
    for a in range(2):
        for b in range(2):
            pl.when(step == a * 2 + b)(functools.partial(body, a, b))


def near_source(r, c):
    rows_in, cols_in = 1 <= r < 5, 1 <= c < 5
    if rows_in and cols_in:
        return "own", None
    if rows_in:
        return "sides", (0 if c == 0 else 4) + r - 1
    if cols_in:
        return "sides", (8 if r == 0 else 12) + c - 1
    return "corners", (0 if r == 0 else 2) + (0 if c == 0 else 1)


CORNER_HALO = [
    n for (t, k), n in HALO.items() if near_source(t // 4 + k // 3, t % 4 + k % 3)[0] == "corners"
]


def near_part(kind, t, tile_of, held):
    r, c = t // 4, t % 4
    made, blocks = [], []
    for k in range(9):
        found, place = near_source(r + k // 3, c + k % 3)
        if found == kind:
            made.append(tile_of(HALO[t, k]))
            blocks.append(held[place])
    if not made:
        return None
    return nn(jnp.concatenate(made, axis=1), jnp.concatenate(blocks, axis=0))


def sides_kernel(
    flags, couplings, field_in, near_a, near_b, halo_a, halo_b, left, right, above, below,
    field, near, held, near_held, halo, sems,
):
    step = pl.program_id(0)

    def copies():
        pairs = [(left.at[0:8], held.at[0:8]), (right.at[0:8], held.at[8:16])]
        for n, src in enumerate((left, right, above, below)):
            pairs.append((src.at[8:12], near_held.at[4 * n : 4 * n + 4]))
        pairs.append((halo_a, halo.at[0:N_HALO]))
        pairs.append((halo_b, halo.at[N_HALO : 2 * N_HALO]))
        return [pltpu.make_async_copy(src, dst, sems.at[n]) for n, (src, dst) in enumerate(pairs)]

    @pl.when(step == 0)
    def _():
        started = copies()
        for copy in started:
            copy.start()
        held[16] = jnp.zeros((256, 256), BF16)
        for copy in started[:2]:
            copy.wait()

    def body(a, b):
        sums = level_zero_sums("sides", a, b, flags, couplings.at[0], held, 16)
        for x, y in PARENTS:
            field[x, 0, y, 0] = field_in[x, 0, y, 0] + sums[x, y]
        if a == 0 and b == 0:
            for copy in copies()[2:]:
                copy.wait()
        for x, y in PARENTS:
            part = near_part("sides", number_of(a, b, (x, y)), lambda n: halo[n], near_held)
            here = (near_b if x else near_a)[0, y, 0]
            near[x, 0, y, 0] = here if part is None else here + part

    each_class(step, body)


HALF_BLOCK = pl.BlockSpec((1, 2, 1, 256, 256), lambda g: (g // 2, 0, g % 2, 0, 0))


def sides_level(flags, couplings, field, near_a, near_b, *received):
    half = lambda x: x.reshape(2, 2, 2, 256, 256)
    return pl.pallas_call(
        sides_kernel,
        grid=(4,),
        out_shape=(GROUPED_F32, GROUPED_F32),
        in_specs=[SMEM_SPEC, COUPLING_BLOCK, CLASS_BLOCK, HALF_BLOCK, HALF_BLOCK] + [ANY_SPEC] * 6,
        out_specs=[CLASS_BLOCK, CLASS_BLOCK],
        scratch_shapes=[
            VMEM((17, 256, 256), BF16),
            VMEM((16, 256, 256), BF16),
            VMEM((2 * N_HALO, 256, 256), BF16),
            pltpu.SemaphoreType.DMA((8,)),
        ],
        compiler_params=params(),
        cost_estimate=cost(300, 30 << 20),
        name="far_sides",
    )(flags, couplings, field, half(near_a), half(near_b), *received)


def last_kernel(
    flags, couplings, t_one, basis, down_one, field, near, halo_a, halo_b, above, below, out,
    held, near_held, halo, sems,
):
    step = pl.program_id(0)

    @pl.when(step == 0)
    def _():
        copies = Copies(sems)
        copies.start(above.at[0:8], held.at[0:8])
        copies.start(below.at[0:8], held.at[8:16])
        copies.start(above.at[8:10], near_held.at[0:2])
        copies.start(below.at[8:10], near_held.at[2:4])
        for m, n in enumerate(CORNER_HALO):
            copies.start((halo_a if n < N_HALO else halo_b).at[n % N_HALO], halo.at[m])
        held[16] = jnp.zeros((256, 256), BF16)
        copies.wait()

    def body(a, b):
        sums = level_zero_sums("corners", a, b, flags, couplings.at[0], held, 16)
        for x, y in PARENTS:
            total = field[x, 0, y, 0] + nt(down_one[x * 2 + y], t_one[x, 0, y, 0])
            if (x, y) in sums:
                total = total + sums[x, y]
            far = nt(basis[x, 0, y, 0], total.astype(BF16))
            near_sum = near[x, 0, y, 0]
            part = near_part(
                "corners",
                number_of(a, b, (x, y)),
                lambda n: halo[CORNER_HALO.index(n)],
                near_held,
            )
            if part is not None:
                near_sum = near_sum + part
            out[x, 0, y, 0] = (near_sum * TILE_SCALE + far).astype(BF16)

    each_class(step, body)


def last_level(flags, couplings, t_one, basis, *rest):
    return pl.pallas_call(
        last_kernel,
        grid=(4,),
        out_shape=jax.ShapeDtypeStruct((2, 2, 2, 2, 256, 256), BF16),
        in_specs=[
            SMEM_SPEC,
            COUPLING_BLOCK,
            CLASS_BLOCK,
            CLASS_BLOCK,
            pl.BlockSpec((4, 256, 256), lambda g: (0, 0, 0)),
            CLASS_BLOCK,
            CLASS_BLOCK,
        ]
        + [ANY_SPEC] * 4,
        out_specs=CLASS_BLOCK,
        scratch_shapes=[
            VMEM((17, 256, 256), BF16),
            VMEM((4, 256, 256), BF16),
            VMEM((len(CORNER_HALO), 256, 256), BF16),
            pltpu.SemaphoreType.DMA((4 + len(CORNER_HALO),)),
        ],
        compiler_params=params(),
        cost_estimate=cost(270, 20 << 20),
        name="last_level",
    )(flags, couplings, grouped(t_one), grouped(basis), *rest)


def per_device(
    positions,
    samples,
    leaf_basis,
    transfer_one,
    transfer_two,
    couplings,
    near_lists,
    far_zero,
    far_one,
    far_two,
):
    nx = lax.axis_size("qx")
    ny = lax.axis_size("qy")
    down_x = [(k, k + 1) for k in range(nx - 1)]
    up_x = [(k + 1, k) for k in range(nx - 1)]
    down_y = [(k, k + 1) for k in range(ny - 1)]
    up_y = [(k + 1, k) for k in range(ny - 1)]

    up, down, left, right, upper, cell = coefficients(
        samples, leaf_basis, transfer_one, transfer_two
    )

    swap_y = [(k, k ^ 1) for k in range(ny)]
    swap_x = [(k, k ^ 1) for k in range(nx)]
    cross_x = [(k, k + 1) for k in range(1, nx - 1, 2)] + [(k + 1, k) for k in range(1, nx - 1, 2)]
    pair = lax.ppermute(upper, "qy", swap_y)
    if nx == 4:
        others = [lax.ppermute(cell, "qx", [(k, k ^ 2) for k in range(nx)])]
    else:
        others = [
            lax.ppermute(cell, "qx", [(k, k + 2) for k in range(nx - 2)]),
            lax.ppermute(cell, "qx", [(k + 2, k) for k in range(nx - 2)]),
        ]
    others_pair = [lax.ppermute(x, "qy", swap_y) for x in others]
    above = lax.ppermute(down, "qx", down_x)
    below = lax.ppermute(up, "qx", up_x)
    sites = positions.reshape(-1, 2, 256)
    flat_samples = samples.reshape(16, 256, 256)
    near_a, halo_a, flags = near_call(
        0, 4 * nx, 4 * ny, near_lists, far_zero, sites, flat_samples
    )
    pair, others_pair, near_a = lax.optimization_barrier((pair, others_pair, near_a))
    outward = [(k, k + 2) for k in range(0, ny - 2, 2)] + [(k + 2, k) for k in range(1, ny - 2, 2)]
    inward = [(k + 2, k) for k in range(0, ny - 2, 2)] + [(k, k + 2) for k in range(1, ny - 2, 2)]
    n_others = len(others)
    quad = [(0, 4, 1), (1, 4, 1)]
    for n in range(n_others):
        quad += [(2 + n, 0, 1), (2 + n_others + n, 0, 1)]
    n_quad = len(quad)
    across, cells = assembled(
        "pair_payload",
        (upper, pair, *others, *others_pair),
        [(1, 0, 4)] + quad,
        [(0, 4 + n_quad), (4, 4 + n_quad)],
    )
    across, above, below, left, right = lax.optimization_barrier(
        (across, above, below, left, right)
    )
    outer = lax.ppermute(across, "qy", outward)
    inner = lax.ppermute(across, "qy", inward)
    on_right = lax.ppermute(left, "qy", up_y)
    on_right, right = lax.optimization_barrier((on_right, right))
    on_left = lax.ppermute(right, "qy", down_y)
    near_b, halo_b, field = near_call(
        8,
        4 * nx,
        4 * ny,
        near_lists,
        far_zero,
        sites,
        flat_samples,
        (flags, couplings, up, down, above, below),
    )
    inner, outer, near_b = lax.optimization_barrier((inner, outer, near_b))
    row, cells_row = assembled(
        "row_payload",
        (upper, pair, outer, inner, cells),
        [(0, 0, 4), (1, 0, 4), (2, 0, 4), (4, 0, n_quad), (2, 4, n_quad), (3, 4, n_quad)],
        [(0, 12), (12, 12 + 3 * n_quad)],
    )
    row_d = lax.ppermute(row, "qx", cross_x)
    row_e = lax.ppermute(row, "qx", swap_x)
    cells_e = lax.ppermute(cells_row, "qx", swap_x)

    down_one = upper_levels(
        ny, far_one, far_two, couplings, transfer_two, row, row_e, row_d, cells_row, cells_e
    )

    on_left, on_right, down_one = lax.optimization_barrier((on_left, on_right, down_one))
    corner_down, corner_up = assembled(
        "corner_payload",
        (on_left, on_right),
        [(0, 4, 4), (1, 4, 4), (0, 11, 1), (1, 11, 1)]
        + [(0, 0, 4), (1, 0, 4), (0, 8, 1), (1, 8, 1)],
        [(0, 10), (10, 20)],
        stated=6000,
    )
    corner_above = lax.ppermute(corner_down, "qx", down_x)
    corner_below = lax.ppermute(corner_up, "qx", up_x)
    field, near = sides_level(
        flags, couplings, grouped(field), near_a, near_b, halo_a, halo_b,
        on_left, on_right, above, below,
    )
    result = last_level(
        flags, couplings, transfer_one, leaf_basis, down_one, field, near, halo_a, halo_b,
        corner_above, corner_below,
    )
    return result.reshape(4, 4, 256, 256)


def solution(mesh):
    return jax.shard_map(
        per_device,
        mesh=mesh,
        in_specs=(
            P(),
            P("qx", "qy", None, None),
            P("qx", "qy", None, None),
            P("qx", "qy", None, None),
            P("qx", "qy", None, None),
            P(),
            P("qx", "qy", None),
            P("qx", "qy", None),
            P("qx", "qy", None),
            P("qx", "qy", None),
        ),
        out_specs=P("qx", "qy", None, None),
        check_vma=False,
    )
```

profile of v0, /device:TPU:17, one launch (start us, length us, event | category | flops | bytes accessed | tf_op | source)
XLA Modules:
  0.0 177.3 jit_solution(14641863299613427779)
XLA Ops:
  0.0 5.4 %coefficients.1 = (bf16[12,256,256]{2,1,0:T(8,128)(2,1)}, bf16[12,256,256]{2,1,0:T(8,128)(2,1)}, bf16[12,256,256]{2,1,0:T(8,128)(2,1)}, bf16[12,256,256]{2,1,0:T...) custom-call(bf16[4,4,256,256]{3,2,1,0:T(8,128)(2,1)} %samples.1, ...), custom_call_target="tpu_custom_call" | custom-call | flops 713031680 | bytes 1572864 | tf_op jit(solution)/shard_map/coefficients/pallas_call | solution.py:145
  5.5 1.3 collective-permute-start.1
  8.0 3.2 %collective-permute-start.3 = (bf16[12,256,256]{2,1,0:T(8,128)(2,1)}, bf16[12,256,256]{2,1,0:T(8,128)(2,1)}, u32[]{:S(2)}, u32[]{:S(2)}) collective-permute-start(bf16[12,256,256]{2,1,0:T(8,128)(2,1)} %get-tuple-element.48.rest_3_), channel_id=1, source_target_pairs={{0,8},{8,16},{16,24},{1,9},{9,17},{17,25},{2,10},{10,18},{18,26},{... | collective-permute-start | bytes 4718600 | tf_op jit(solution)/shard_map/ppermute | solution.py:779
  11.2 2.8 %collective-permute-start.4 = (bf16[12,256,256]{2,1,0:T(8,128)(2,1)}, bf16[12,256,256]{2,1,0:T(8,128)(2,1)}, u32[]{:S(2)}, u32[]{:S(2)}) collective-permute-start(bf16[12,256,256]{2,1,0:T(8,128)(2,1)} %get-tuple-element.49.rest_2_), channel_id=1, source_target_pairs={{8,0},{16,8},{24,16},{9,1},{17,9},{25,17},{10,2},{18,10},{26,18},{... | collective-permute-start | bytes 4718600 | tf_op jit(solution)/shard_map/ppermute | solution.py:780
  14.4 13.7 %near_first.1 = (f32[8,256,256]{2,1,0:T(8,128)}, bf16[22,256,256]{2,1,0:T(8,128)(2,1)}, s32[16,37]{1,0:T(8,128)}) custom-call(s32[4,4,9]{2,1,0:T(4,128)} %lists.3, s32[4,4,27]{2,1,0:T(4,128)} %far_zero.3, f32[512,2,256]{2,1,0:T(2,128)} %bitcast.15, bf16[16,256,256]{2,1,0:T(8,128)(2,1)} %bitcast.8), custom_call_target="tpu_custom_call" | custom-call | flops 50331648000 | bytes 1048576 | tf_op jit(solution)/shard_map/near_first/pallas_call | solution.py:373
  28.1 2.5 %pair_payload.1 = (bf16[8,256,256]{2,1,0:T(8,128)(2,1)}, bf16[4,256,256]{2,1,0:T(8,128)(2,1)}) custom-call(bf16[5,256,256]{2,1,0:T(8,128)(2,1)} %get-tuple-element.42.refs_0_, bf16[5,256,256]{2,1,0:T(8,128)(2,1)} %collective-permute-done.refs_1_, bf16[1,256,256]{2,1,0:T(8,128)(2,1)} %copy-done, bf16[1,256,256]{2,1,0:T(8,128)(2,1)} %collective-permute-done.2.refs_3_), custom_call_target="tpu_custom_call" | custom-call | flops 146800640 | tf_op jit(solution)/shard_map/pair_payload/pallas_call | solution.py:183
  30.6 2.7 %collective-permute-done.4.rest_5_.below = bf16[12,256,256]{2,1,0:T(8,128)(2,1)} collective-permute-done((bf16[12,256,256]{2,1,0:T(8,128)(2,1)}, bf16[12,256,256]{2,1,0:T(8,128)(2,1)}, u32[]{:S(2)}, u32[]{:S(2)}) %collective-permute-start.4) | collective-permute-done | bytes 1572896 | tf_op jit(solution)/shard_map/ppermute | solution.py:780
  33.3 2.0 %collective-permute-start.5 = (bf16[12,256,256]{2,1,0:T(8,128)(2,1)}, bf16[12,256,256]{2,1,0:T(8,128)(2,1)}, u32[]{:S(2)}, u32[]{:S(2)}) collective-permute-start(bf16[12,256,256]{2,1,0:T(8,128)(2,1)} %get-tuple-element.52), channel_id=1, source_target_pairs={{1,0},{2,1},{3,2},{4,3},{5,4},{6,5},{7,6},{9,8},{10,9},{11,10},{12... | collective-permute-start | bytes 4718600 | tf_op jit(solution)/shard_map/ppermute | solution.py:805
  35.3 2.0 %collective-permute-start.7 = (bf16[8,256,256]{2,1,0:T(8,128)(2,1)}, bf16[8,256,256]{2,1,0:T(8,128)(2,1)}, u32[]{:S(2)}, u32[]{:S(2)}) collective-permute-start(bf16[8,256,256]{2,1,0:T(8,128)(2,1)} %get-tuple-element.56), channel_id=1, source_target_pairs={{2,0},{4,2},{6,4},{1,3},{3,5},{5,7},{10,8},{12,10},{14,12},{9,11},... | collective-permute-start | bytes 3145736 | tf_op jit(solution)/shard_map/ppermute | solution.py:804
  37.3 4.3 %collective-permute-start.8 = (bf16[8,256,256]{2,1,0:T(8,128)(2,1)}, bf16[8,256,256]{2,1,0:T(8,128)(2,1)}, u32[]{:S(2)}, u32[]{:S(2)}) collective-permute-start(bf16[8,256,256]{2,1,0:T(8,128)(2,1)} %get-tuple-element.56), channel_id=1, source_target_pairs={{0,2},{2,4},{4,6},{3,1},{5,3},{7,5},{8,10},{10,12},{12,14},{11,9},... | collective-permute-start | bytes 3145736 | tf_op jit(solution)/shard_map/ppermute | solution.py:803
  41.6 19.9 %near_and_inner_far.1 = (f32[8,256,256]{2,1,0:T(8,128)}, bf16[22,256,256]{2,1,0:T(8,128)(2,1)}, f32[16,256,256]{2,1,0:T(8,128)}) custom-call(s32[4,4,9]{2,1,0:T(4,128)} %lists.3, s32[4,4,27]{2,1,0:T(4,128)} %far_zero.3, f32[512,2,256]{2,1,0:T(2,128)} %bitcast.16, bf16[16,256,256]{2,1,0:T(8,128)(2,1)} %bitcast.9, s32[16,37]{1,0:T(8,128)} %get-tuple-element.41.rest_0_.flags, ...), custom_call_target="tpu_custom_call" | custom-call | flops 2516582400 | bytes 1048576 | tf_op jit(solution)/shard_map/near_and_inner_far/pallas_call | solution.py:373
  61.5 31.0 %collective-permute-done.7.refs_3_ = bf16[8,256,256]{2,1,0:T(8,128)(2,1)} collective-permute-done((bf16[8,256,256]{2,1,0:T(8,128)(2,1)}, bf16[8,256,256]{2,1,0:T(8,128)(2,1)}, u32[]{:S(2)}, u32[]{:S(2)}) %collective-permute-start.7) | collective-permute-done | bytes 1048608 | tf_op jit(solution)/shard_map/ppermute | solution.py:804
  92.5 3.6 %row_payload.1 = (bf16[12,256,256]{2,1,0:T(8,128)(2,1)}, bf16[12,256,256]{2,1,0:T(8,128)(2,1)}) custom-call(bf16[5,256,256]{2,1,0:T(8,128)(2,1)} %get-tuple-element.42.refs_0_, bf16[5,256,256]{2,1,0:T(8,128)(2,1)} %collective-permute-done.refs_1_, bf16[8,256,256]{2,1,0:T(8,128)(2,1)} %collective-permute-done.8.refs_2_, ...), custom_call_target="tpu_custom_call" | custom-call | flops 146800640 | tf_op jit(solution)/shard_map/row_payload/pallas_call | solution.py:183
  96.2 3.2 %collective-permute-start.10 = (bf16[12,256,256]{2,1,0:T(8,128)(2,1)}, bf16[12,256,256]{2,1,0:T(8,128)(2,1)}, u32[]{:S(2)}, u32[]{:S(2)}) collective-permute-start(bf16[12,256,256]{2,1,0:T(8,128)(2,1)} %get-tuple-element.63.row), channel_id=1, source_target_pairs={{8,16},{16,8},{9,17},{17,9},{10,18},{18,10},{11,19},{19,11},{12,20... | collective-permute-start | bytes 4718600 | tf_op jit(solution)/shard_map/ppermute | solution.py:825
  99.5 1.9 %collective-permute-start.6 = (bf16[12,256,256]{2,1,0:T(8,128)(2,1)}, bf16[12,256,256]{2,1,0:T(8,128)(2,1)}, u32[]{:S(2)}, u32[]{:S(2)}) collective-permute-start(bf16[12,256,256]{2,1,0:T(8,128)(2,1)} %get-tuple-element.54), channel_id=1, source_target_pairs={{0,1},{1,2},{2,3},{3,4},{4,5},{5,6},{6,7},{8,9},{9,10},{10,11},{11... | collective-permute-start | bytes 4718600 | tf_op jit(solution)/shard_map/ppermute | solution.py:807
  101.5 17.1 %collective-permute-done.10.row_d = bf16[12,256,256]{2,1,0:T(8,128)(2,1)} collective-permute-done((bf16[12,256,256]{2,1,0:T(8,128)(2,1)}, bf16[12,256,256]{2,1,0:T(8,128)(2,1)}, u32[]{:S(2)}, u32[]{:S(2)}) %collective-permute-start.10) | collective-permute-done | bytes 1572896 | tf_op jit(solution)/shard_map/ppermute | solution.py:825
  118.6 10.7 %upper_levels.1.down_one = bf16[4,256,256]{2,1,0:T(8,128)(2,1)} custom-call(s32[2,2,27]{2,1,0:T(2,128)} %far_one.1, s32[1,1,27]{2,1,0:T(1,128)} %far_two.1, bf16[3,20,256,256]{3,2,1,0:T(8,128)(2,1)} %couplings.5, bf16[2,2,256,256]{3,2,1,0:T(8,128)(2,1)} %t_two.3, bf16[12,256,256]{2,1,0:T(8,128)(2,1)} %get-tuple-element.63.row, ...), custom_call_target="tpu_custom_call" | custom-call | flops 1426063360 | bytes 1835008 | tf_op jit(solution)/shard_map/upper_levels/pallas_call | solution.py:501
  129.3 8.9 %collective-permute-done.6.left.refs_0_ = bf16[12,256,256]{2,1,0:T(8,128)(2,1)} collective-permute-done((bf16[12,256,256]{2,1,0:T(8,128)(2,1)}, bf16[12,256,256]{2,1,0:T(8,128)(2,1)}, u32[]{:S(2)}, u32[]{:S(2)}) %collective-permute-start.6) | collective-permute-done | bytes 1572896 | tf_op jit(solution)/shard_map/ppermute | solution.py:807
  138.1 3.2 %corner_payload.1 = (bf16[10,256,256]{2,1,0:T(8,128)(2,1)}, bf16[10,256,256]{2,1,0:T(8,128)(2,1)}) custom-call(bf16[12,256,256]{2,1,0:T(8,128)(2,1)} %collective-permute-done.6.left.refs_0_, bf16[12,256,256]{2,1,0:T(8,128)(2,1)} %collective-permute-done.5.right.refs_1_), custom_call_target="tpu_custom_call" | custom-call | flops 25165824000 | tf_op jit(solution)/shard_map/corner_payload/pallas_call | solution.py:183
  141.4 3.6 %collective-permute-start.12 = (bf16[10,256,256]{2,1,0:T(8,128)(2,1)}, bf16[10,256,256]{2,1,0:T(8,128)(2,1)}, u32[]{:S(2)}, u32[]{:S(2)}) collective-permute-start(bf16[10,256,256]{2,1,0:T(8,128)(2,1)} %get-tuple-element.75), channel_id=1, source_target_pairs={{0,8},{8,16},{16,24},{1,9},{9,17},{17,25},{2,10},{10,18},{18,26},{... | collective-permute-start | bytes 3932168 | tf_op jit(solution)/shard_map/ppermute | solution.py:842
  145.0 1.9 %collective-permute-start.13 = (bf16[10,256,256]{2,1,0:T(8,128)(2,1)}, bf16[10,256,256]{2,1,0:T(8,128)(2,1)}, u32[]{:S(2)}, u32[]{:S(2)}) collective-permute-start(bf16[10,256,256]{2,1,0:T(8,128)(2,1)} %get-tuple-element.76), channel_id=1, source_target_pairs={{8,0},{16,8},{24,16},{9,1},{17,9},{25,17},{10,2},{18,10},{26,18},{... | collective-permute-start | bytes 3932168 | tf_op jit(solution)/shard_map/ppermute | solution.py:843
  146.9 14.2 %far_sides.1 = (f32[2,2,2,2,256,256]{5,4,3,2,1,0:T(8,128)}, f32[2,2,2,2,256,256]{5,4,3,2,1,0:T(8,128)}) custom-call(s32[16,37]{1,0:T(8,128)} %get-tuple-element.41.rest_0_.flags, bf16[3,20,256,256]{3,2,1,0:T(8,128)(2,1)} %couplings.5, f32[2,2,2,2,256,256]{5,4,3,2,1,0:T(8,128)} %bitcast.12, f32[2,2,2,256,256]{4,3,2,1,0:T(8,128)} %bitcast.13, ...), custom_call_target="tpu_custom_call" | custom-call | flops 1258291200 | bytes 3932160 | tf_op jit(solution)/shard_map/far_sides/pallas_call | solution.py:659
  161.2 3.0 %collective-permute-done.13.below = bf16[10,256,256]{2,1,0:T(8,128)(2,1)} collective-permute-done((bf16[10,256,256]{2,1,0:T(8,128)(2,1)}, bf16[10,256,256]{2,1,0:T(8,128)(2,1)}, u32[]{:S(2)}, u32[]{:S(2)}) %collective-permute-start.13) | collective-permute-done | bytes 1310752 | tf_op jit(solution)/shard_map/ppermute | solution.py:843
  164.2 12.7 %last_level.1 = bf16[2,2,2,2,256,256]{5,4,3,2,1,0:T(8,128)(2,1)} custom-call(s32[16,37]{1,0:T(8,128)} %get-tuple-element.41.rest_0_.flags, bf16[3,20,256,256]{3,2,1,0:T(8,128)(2,1)} %couplings.5, bf16[2,2,2,2,256,256]{5,4,3,2,1,0:T(8,128)(2,1)} %bitcast.10, bf16[2,2,2,2,256,256]{5,4,3,2,1,0:T(8,128)(2,1)} %bitcast.11, ...), custom_call_target="tpu_custom_call" | custom-call | flops 1132462080 | bytes 2621440 | tf_op jit(solution)/shard_map/last_level/pallas_call | solution.py:717
  (15 shorter events, 1.7 us)
Async XLA Ops:
  5.5 8.6 %collective-permute-start.1 = (bf16[1,256,256]{2,1,0:T(8,128)(2,1)}, bf16[1,256,256]{2,1,0:T(8,128)(2,1)S(1)}, u32[]{:S(2)}, u32[]{:S(2)}) collective-permute-start(bf16[1,256,256]{2,1,0:T(8,128)(2,1)} %get-tuple-element.43), channel_id=1, source_target_pairs={{0,16},{8,24},{16,0},{24,8},{1,17},{9,25},{17,1},{25,9},{2,18},{10... | collective-permute-start | bytes 393224 | tf_op jit(solution)/shard_map/ppermute | solution.py:772
  6.8 21.4 %collective-permute-start = (bf16[5,256,256]{2,1,0:T(8,128)(2,1)}, bf16[5,256,256]{2,1,0:T(8,128)(2,1)}, u32[]{:S(2)}, u32[]{:S(2)}) collective-permute-start(bf16[5,256,256]{2,1,0:T(8,128)(2,1)} %get-tuple-element.42.refs_0_), channel_id=1, source_target_pairs={{0,1},{1,0},{2,3},{3,2},{4,5},{5,4},{6,7},{7,6},{8,9},{9,8},{10,11... | collective-permute-start | bytes 1966088 | tf_op jit(solution)/shard_map/ppermute | solution.py:770
  8.0 22.6 %collective-permute-start.3 = (bf16[12,256,256]{2,1,0:T(8,128)(2,1)}, bf16[12,256,256]{2,1,0:T(8,128)(2,1)}, u32[]{:S(2)}, u32[]{:S(2)}) collective-permute-start(bf16[12,256,256]{2,1,0:T(8,128)(2,1)} %get-tuple-element.48.rest_3_), channel_id=1, source_target_pairs={{0,8},{8,16},{16,24},{1,9},{9,17},{17,25},{2,10},{10,18},{18,26},{... | collective-permute-start | bytes 4718600 | tf_op jit(solution)/shard_map/ppermute | solution.py:779
  11.2 22.1 %collective-permute-start.4 = (bf16[12,256,256]{2,1,0:T(8,128)(2,1)}, bf16[12,256,256]{2,1,0:T(8,128)(2,1)}, u32[]{:S(2)}, u32[]{:S(2)}) collective-permute-start(bf16[12,256,256]{2,1,0:T(8,128)(2,1)} %get-tuple-element.49.rest_2_), channel_id=1, source_target_pairs={{8,0},{16,8},{24,16},{9,1},{17,9},{25,17},{10,2},{18,10},{26,18},{... | collective-permute-start | bytes 4718600 | tf_op jit(solution)/shard_map/ppermute | solution.py:780
  14.1 14.0 %copy-start = (bf16[1,256,256]{2,1,0:T(8,128)(2,1)}, bf16[1,256,256]{2,1,0:T(8,128)(2,1)S(1)}, u32[]{:S(2)}) copy-start(bf16[1,256,256]{2,1,0:T(8,128)(2,1)S(1)} %collective-permute-done.1.refs_2_) | copy-start | bytes 393220
  14.1 14.0 %collective-permute-start.2 = (bf16[1,256,256]{2,1,0:T(8,128)(2,1)S(1)}, bf16[1,256,256]{2,1,0:T(8,128)(2,1)}, u32[]{:S(2)}, u32[]{:S(2)}) collective-permute-start(bf16[1,256,256]{2,1,0:T(8,128)(2,1)S(1)} %collective-permute-done.1.refs_2_), channel_id=1, source_target_pairs={{0,1},{1,0},{2,3},{3,2},{4,5},{5,4},{6,7},{7,6},{8,9},{9,8},{10,11... | collective-permute-start | bytes 393224 | tf_op jit(solution)/shard_map/ppermute | solution.py:778
  33.3 66.3 %collective-permute-start.5 = (bf16[12,256,256]{2,1,0:T(8,128)(2,1)}, bf16[12,256,256]{2,1,0:T(8,128)(2,1)}, u32[]{:S(2)}, u32[]{:S(2)}) collective-permute-start(bf16[12,256,256]{2,1,0:T(8,128)(2,1)} %get-tuple-element.52), channel_id=1, source_target_pairs={{1,0},{2,1},{3,2},{4,3},{5,4},{6,5},{7,6},{9,8},{10,9},{11,10},{12... | collective-permute-start | bytes 4718600 | tf_op jit(solution)/shard_map/ppermute | solution.py:805
  35.3 57.2 %collective-permute-start.7 = (bf16[8,256,256]{2,1,0:T(8,128)(2,1)}, bf16[8,256,256]{2,1,0:T(8,128)(2,1)}, u32[]{:S(2)}, u32[]{:S(2)}) collective-permute-start(bf16[8,256,256]{2,1,0:T(8,128)(2,1)} %get-tuple-element.56), channel_id=1, source_target_pairs={{2,0},{4,2},{6,4},{1,3},{3,5},{5,7},{10,8},{12,10},{14,12},{9,11},... | collective-permute-start | bytes 3145736 | tf_op jit(solution)/shard_map/ppermute | solution.py:804
  37.3 55.2 %collective-permute-start.8 = (bf16[8,256,256]{2,1,0:T(8,128)(2,1)}, bf16[8,256,256]{2,1,0:T(8,128)(2,1)}, u32[]{:S(2)}, u32[]{:S(2)}) collective-permute-start(bf16[8,256,256]{2,1,0:T(8,128)(2,1)} %get-tuple-element.56), channel_id=1, source_target_pairs={{0,2},{2,4},{4,6},{3,1},{5,3},{7,5},{8,10},{10,12},{12,14},{11,9},... | collective-permute-start | bytes 3145736 | tf_op jit(solution)/shard_map/ppermute | solution.py:803
  96.1 5.3 %collective-permute-start.9 = (bf16[12,256,256]{2,1,0:T(8,128)(2,1)}, bf16[12,256,256]{2,1,0:T(8,128)(2,1)}, u32[]{:S(2)}, u32[]{:S(2)}) collective-permute-start(bf16[12,256,256]{2,1,0:T(8,128)(2,1)} %get-tuple-element.63.row), channel_id=1, source_target_pairs={{0,8},{8,0},{16,24},{24,16},{1,9},{9,1},{17,25},{25,17},{2,10},{10... | collective-permute-start | bytes 4718600 | tf_op jit(solution)/shard_map/ppermute | solution.py:826
  96.2 22.3 %collective-permute-start.10 = (bf16[12,256,256]{2,1,0:T(8,128)(2,1)}, bf16[12,256,256]{2,1,0:T(8,128)(2,1)}, u32[]{:S(2)}, u32[]{:S(2)}) collective-permute-start(bf16[12,256,256]{2,1,0:T(8,128)(2,1)} %get-tuple-element.63.row), channel_id=1, source_target_pairs={{8,16},{16,8},{9,17},{17,9},{10,18},{18,10},{11,19},{19,11},{12,20... | collective-permute-start | bytes 4718600 | tf_op jit(solution)/shard_map/ppermute | solution.py:825
  99.4 19.1 %collective-permute-start.11 = (bf16[12,256,256]{2,1,0:T(8,128)(2,1)}, bf16[12,256,256]{2,1,0:T(8,128)(2,1)}, u32[]{:S(2)}, u32[]{:S(2)}) collective-permute-start(bf16[12,256,256]{2,1,0:T(8,128)(2,1)} %get-tuple-element.64.cells), channel_id=1, source_target_pairs={{0,8},{8,0},{16,24},{24,16},{1,9},{9,1},{17,25},{25,17},{2,10},{10... | collective-permute-start | bytes 4718600 | tf_op jit(solution)/shard_map/ppermute | solution.py:827
  99.5 38.6 %collective-permute-start.6 = (bf16[12,256,256]{2,1,0:T(8,128)(2,1)}, bf16[12,256,256]{2,1,0:T(8,128)(2,1)}, u32[]{:S(2)}, u32[]{:S(2)}) collective-permute-start(bf16[12,256,256]{2,1,0:T(8,128)(2,1)} %get-tuple-element.54), channel_id=1, source_target_pairs={{0,1},{1,2},{2,3},{3,4},{4,5},{5,6},{6,7},{8,9},{9,10},{10,11},{11... | collective-permute-start | bytes 4718600 | tf_op jit(solution)/shard_map/ppermute | solution.py:807
  141.4 19.8 %collective-permute-start.12 = (bf16[10,256,256]{2,1,0:T(8,128)(2,1)}, bf16[10,256,256]{2,1,0:T(8,128)(2,1)}, u32[]{:S(2)}, u32[]{:S(2)}) collective-permute-start(bf16[10,256,256]{2,1,0:T(8,128)(2,1)} %get-tuple-element.75), channel_id=1, source_target_pairs={{0,8},{8,16},{16,24},{1,9},{9,17},{17,25},{2,10},{10,18},{18,26},{... | collective-permute-start | bytes 3932168 | tf_op jit(solution)/shard_map/ppermute | solution.py:842
  145.0 19.2 %collective-permute-start.13 = (bf16[10,256,256]{2,1,0:T(8,128)(2,1)}, bf16[10,256,256]{2,1,0:T(8,128)(2,1)}, u32[]{:S(2)}, u32[]{:S(2)}) collective-permute-start(bf16[10,256,256]{2,1,0:T(8,128)(2,1)} %get-tuple-element.76), channel_id=1, source_target_pairs={{8,0},{16,8},{24,16},{9,1},{17,9},{25,17},{10,2},{18,10},{26,18},{... | collective-permute-start | bytes 3932168 | tf_op jit(solution)/shard_map/ppermute | solution.py:843
where the time goes:
time: 180 us; the launch traced here: 177 us
  Pallas kernels  86 us (48%)
  waiting for transfers between devices  62.6 us (35%)
  starting transfers between devices  28.1 us (16%)
    pallas_call x2, Pallas kernels, near_call(): pl.pallas_call(functools.partial(near_kernel, first, bool(far), grid_rows...  33.6 us
    ppermute x1, waiting for transfers between devices, per_device(): inner = lax.ppermute(across, 'qy', inward)  31 us
    ppermute x1, waiting for transfers between devices, per_device(): row_d = lax.ppermute(row, 'qx', cross_x)  17.1 us
    pallas_call x1, Pallas kernels, sides_level(): pl.pallas_call(sides_kernel, grid=(4,), out_shape=(GROUPED_F32, GROUPED_F...  14.2 us
    pallas_call x1, Pallas kernels, last_level(): pl.pallas_call(last_kernel, grid=(4,), out_shape=jax.ShapeDtypeStruct((2,...  12.7 us
    pallas_call x1, Pallas kernels, upper_levels(): pl.pallas_call(functools.partial(upper_kernel, grid_cols, n_two // 6), gr...  10.7 us
    pallas_call x3, Pallas kernels, assembled(): pl.pallas_call(kernel, out_shape=[tiles(last - first) for first, last in...  9.33 us
    ppermute x1, waiting for transfers between devices, per_device(): on_left = lax.ppermute(right, 'qy', down_y)  8.87 us
  transfers between devices with their start and end apart: 14, of which 5 were waited for; matrix products, arithmetic and copies ran while one was open for 0% of the time, Pallas kernels for 36%

commit v1 on v0

--- a/solution.py
+++ b/solution.py
@@ -136,6 +136,8 @@
     lhs = jnp.concatenate([uv[k] for k in range(4)], axis=1)
     rhs = jnp.concatenate([t2v[k // 2, k % 2] for k in range(4)], axis=0)
     uv[4] = nn(lhs, rhs).astype(BF16)
+    out.start(uv.at[0:4], up.at[12:16])
+    out.start(uv.at[0:4], down.at[12:16])
     out.start(uv, upper)
     out.start(uv.at[4:5], cell)
     out.wait()
@@ -144,7 +146,7 @@
 def coefficients(samples, basis, t_one, t_two):
     return pl.pallas_call(
         coef_kernel,
-        out_shape=[tiles(n) for n in (12, 12, 12, 12, 5, 1)],
+        out_shape=[tiles(n) for n in (16, 16, 12, 12, 5, 1)],
         in_specs=[ANY_SPEC] * 4,
         out_specs=[ANY_SPEC] * 6,
         scratch_shapes=[
@@ -155,7 +157,7 @@
             VMEM((16, 256, 256), BF16),
             VMEM((5, 256, 256), BF16),
             pltpu.SemaphoreType.DMA((13,)),
-            pltpu.SemaphoreType.DMA((24,)),
+            pltpu.SemaphoreType.DMA((26,)),
         ],
         compiler_params=params(),
         cost_estimate=cost(170, 12 << 20),
@@ -427,17 +429,23 @@
 
 
 def upper_kernel(
-    grid_cols, n_rows, far_one, far_two, couplings, t_two, row, row_e, row_d, cells, cells_e, down,
-    held_one, held_two, field_two, flags, sems,
+    grid_cols, n_rows, far_one, far_two, couplings, t_two, upper, above, below, row, row_e, row_d,
+    cells, cells_e, quads, quads_e, down, held_one, held_two, field_two, flags, sems,
 ):
-    n_two = 6 * n_rows
+    n_cells = 2 * n_rows
+    n_two = 3 * n_cells
     zero_one, zero_two = 36, 2 * n_two
     copies = Copies(sems)
-    copies.start(cells, held_two.at[0:n_two])
-    copies.start(cells_e, held_two.at[n_two : 2 * n_two])
-    copies.start(row, held_one.at[0:12])
-    copies.start(row_e, held_one.at[12:24])
-    copies.start(row_d, held_one.at[24:36])
+    copies.start(cells, held_two.at[0:n_cells])
+    copies.start(quads, held_two.at[n_cells:n_two])
+    copies.start(cells_e, held_two.at[n_two : n_two + n_cells])
+    copies.start(quads_e, held_two.at[n_two + n_cells : 2 * n_two])
+    copies.start(upper.at[0:4], held_one.at[0:4])
+    copies.start(row, held_one.at[4:12])
+    copies.start(above.at[12:16], held_one.at[12:16])
+    copies.start(below.at[12:16], held_one.at[16:20])
+    copies.start(row_e, held_one.at[20:28])
+    copies.start(row_d, held_one.at[28:36])
     held_one[zero_one] = jnp.zeros((256, 256), BF16)
     held_two[zero_two] = jnp.zeros((256, 256), BF16)
     i = lax.axis_index("qx")
@@ -466,15 +474,17 @@
         place = core_at[r % 2] + y_at[r // 2] + z_at[c // 2] + x_at[c % 2]
         return jnp.where(flags[4, w] == 1, place, zero_two)
 
-    row_at = [jnp.where(a == 0, 24, 12), 0, jnp.where(a == 0, 12, 24)]
-    col_at = [jnp.where(b == 0, 8, 4), 0, jnp.where(b == 0, 4, 8)]
+    own_at = [12, 0, 16]
+    pair_at = [jnp.where(a == 0, 28, 20), 4, jnp.where(a == 0, 20, 28)]
+    col_at = [jnp.where(b == 0, 4, 0), None, jnp.where(b == 0, 0, 4)]
 
     def place_one(t, w):
         r, c = w // 6, w % 6
-        place = row_at[r // 2] + col_at[c // 2] + (r % 2) * 2 + c % 2
+        base = own_at[r // 2] if c // 2 == 1 else pair_at[r // 2] + col_at[c // 2]
+        place = base + (r % 2) * 2 + c % 2
         return jnp.where(flags[t, w] == 1, place, zero_one)
 
-    for copy in copies.started[:2]:
+    for copy in copies.started[:4]:
         copy.wait()
     for u in range(2):
         for v in range(2):
@@ -485,7 +495,7 @@
                     class_plan(u, v), couplings.at[1], held_two, place_two
                 ).astype(BF16)
 
-    for copy in copies.started[2:]:
+    for copy in copies.started[4:]:
         copy.wait()
     for u in range(2):
         for v in range(2):
@@ -496,8 +506,8 @@
             down[t] = (field + nt(field_two[...], t_two[u, v])).astype(BF16)
 
 
-def upper_levels(grid_cols, far_one, far_two, couplings, t_two, row, row_e, row_d, cells, cells_e):
-    n_two = cells.shape[0]
+def upper_levels(grid_cols, far_one, far_two, couplings, t_two, *received):
+    n_two = 3 * received[6].shape[0]
     return pl.pallas_call(
         functools.partial(upper_kernel, grid_cols, n_two // 6),
         grid=(1,),
@@ -511,19 +521,19 @@
             ),
             pl.BlockSpec((2, 2, 256, 256), lambda g: (0, 0, 0, 0)),
         ]
-        + [ANY_SPEC] * 5,
+        + [ANY_SPEC] * 10,
         out_specs=pl.BlockSpec((4, 256, 256), lambda g: (0, 0, 0)),
         scratch_shapes=[
             VMEM((37, 256, 256), BF16),
             VMEM((2 * n_two + 1, 256, 256), BF16),
             VMEM((256, 256), BF16),
             pltpu.SMEM((5, 37), jnp.int32),
-            pltpu.SemaphoreType.DMA((5,)),
+            pltpu.SemaphoreType.DMA((10,)),
         ],
         compiler_params=params(),
         cost_estimate=cost(340, 14 << 20),
         name="upper_levels",
-    )(far_one, far_two, couplings, t_two, row, row_e, row_d, cells, cells_e)
+    )(far_one, far_two, couplings, t_two, *received)
 
 
 def source_of(x, y, w):
@@ -797,14 +807,12 @@
         [(1, 0, 4)] + quad,
         [(0, 4 + n_quad), (4, 4 + n_quad)],
     )
-    across, above, below, left, right = lax.optimization_barrier(
-        (across, above, below, left, right)
-    )
+    across, cells, left, right = lax.optimization_barrier((across, cells, left, right))
     outer = lax.ppermute(across, "qy", outward)
-    inner = lax.ppermute(across, "qy", inward)
+    inner = lax.ppermute(cells, "qy", inward)
+    cells_e = lax.ppermute(cells, "qx", swap_x)
+    on_left = lax.ppermute(right, "qy", down_y)
     on_right = lax.ppermute(left, "qy", up_y)
-    on_right, right = lax.optimization_barrier((on_right, right))
-    on_left = lax.ppermute(right, "qy", down_y)
     near_b, halo_b, field = near_call(
         8,
         4 * nx,
@@ -816,18 +824,18 @@
         (flags, couplings, up, down, above, below),
     )
     inner, outer, near_b = lax.optimization_barrier((inner, outer, near_b))
-    row, cells_row = assembled(
+    row, quads = assembled(
         "row_payload",
-        (upper, pair, outer, inner, cells),
-        [(0, 0, 4), (1, 0, 4), (2, 0, 4), (4, 0, n_quad), (2, 4, n_quad), (3, 4, n_quad)],
-        [(0, 12), (12, 12 + 3 * n_quad)],
+        (pair, outer, inner),
+        [(0, 0, 4), (1, 0, 4), (1, 4, n_quad), (2, 0, n_quad)],
+        [(0, 8), (8, 8 + 2 * n_quad)],
     )
     row_d = lax.ppermute(row, "qx", cross_x)
     row_e = lax.ppermute(row, "qx", swap_x)
-    cells_e = lax.ppermute(cells_row, "qx", swap_x)
-
+    quads_e = lax.ppermute(quads, "qx", swap_x)
     down_one = upper_levels(
-        ny, far_one, far_two, couplings, transfer_two, row, row_e, row_d, cells_row, cells_e
+        ny, far_one, far_two, couplings, transfer_two, upper, above, below, row, row_e, row_d,
+        cells, cells_e, quads, quads_e,
     )
 
     on_left, on_right, down_one = lax.optimization_barrier((on_left, on_right, down_one))
@@ -837,7 +845,7 @@
         [(0, 4, 4), (1, 4, 4), (0, 11, 1), (1, 11, 1)]
         + [(0, 0, 4), (1, 0, 4), (0, 8, 1), (1, 8, 1)],
         [(0, 10), (10, 20)],
-        stated=6000,
+        stated=35,
     )
     corner_above = lax.ppermute(corner_down, "qx", down_x)
     corner_below = lax.ppermute(corner_up, "qx", up_x)

time: 180 us -> 156 us (0.87)
  waiting for transfers between devices: 62.6 us -> 34.2 us
  starting transfers between devices: 28.1 us -> 32.3 us
    ppermute x2 -> x3, waiting for transfers between devices: 31 us -> 0.01 us  [the longest x1 0.01 us: per_device(): inner = lax.ppermute(cells, 'qy', inward)]
    ppermute x1, waiting for transfers between devices: 8.87 us -> 14.2 us  [per_device(): on_left = lax.ppermute(right, 'qy', down_y)]
    ppermute x1, waiting for transfers between devices: 17.1 us -> 13.2 us  [per_device(): row_d = lax.ppermute(row, 'qx', cross_x)]
    ppermute x1, waiting for transfers between devices: 0.01 us -> 3.81 us  [per_device(): on_right = lax.ppermute(left, 'qy', up_y)]
    ppermute x1, waiting for transfers between devices: 2.65 us -> 0.01 us  [per_device(): below = lax.ppermute(up, 'qx', up_x)]
    ppermute x1, starting transfers between devices: 1.92 us -> 4.06 us  [per_device(): on_left = lax.ppermute(right, 'qy', down_y)]
  transfers between devices with their start and end apart: 14 -> 15, of which waited for: 5 -> 4; matrix products, arithmetic and copies ran while one was open for 0% -> 0% of each run, Pallas kernels for 36% -> 42%
where the time goes in v1:
time: 156 us; the launch traced here: 153 us
  Pallas kernels  85.6 us (55%)
  waiting for transfers between devices  34.2 us (22%)
  starting transfers between devices  32.3 us (21%)
    pallas_call x2, Pallas kernels, near_call(): pl.pallas_call(functools.partial(near_kernel, first, bool(far), grid_rows...  33.6 us
    pallas_call x1, Pallas kernels, sides_level(): pl.pallas_call(sides_kernel, grid=(4,), out_shape=(GROUPED_F32, GROUPED_F...  14.2 us
    ppermute x1, waiting for transfers between devices, per_device(): on_left = lax.ppermute(right, 'qy', down_y)  14.2 us
    ppermute x1, waiting for transfers between devices, per_device(): row_d = lax.ppermute(row, 'qx', cross_x)  13.2 us
    pallas_call x1, Pallas kernels, last_level(): pl.pallas_call(last_kernel, grid=(4,), out_shape=jax.ShapeDtypeStruct((2,...  12.7 us
    pallas_call x1, Pallas kernels, upper_levels(): pl.pallas_call(functools.partial(upper_kernel, grid_cols, n_two // 6), gr...  10.7 us
    pallas_call x3, Pallas kernels, assembled(): pl.pallas_call(kernel, out_shape=[tiles(last - first) for first, last in...  8.49 us
    pallas_call x1, Pallas kernels, coefficients(): pl.pallas_call(coef_kernel, out_shape=[tiles(n) for n in (16, 16, 12, 12,...  5.8 us
  transfers between devices with their start and end apart: 15, of which 4 were waited for; matrix products, arithmetic and copies ran while one was open for 0% of the time, Pallas kernels for 42%

profile of v1, /device:TPU:17, one launch (start us, length us, event | category | flops | bytes accessed | tf_op | source)
XLA Modules:
  0.0 152.6 jit_solution(8826213416391319789)
XLA Ops:
  0.0 5.8 %coefficients.1 = (bf16[16,256,256]{2,1,0:T(8,128)(2,1)}, bf16[16,256,256]{2,1,0:T(8,128)(2,1)}, bf16[12,256,256]{2,1,0:T(8,128)(2,1)}, bf16[12,256,256]{2,1,0:T...) custom-call(bf16[4,4,256,256]{3,2,1,0:T(8,128)(2,1)} %samples.1, ...), custom_call_target="tpu_custom_call" | custom-call | flops 713031680 | bytes 1572864 | tf_op jit(solution)/shard_map/coefficients/pallas_call | solution.py:147
  5.8 1.3 collective-permute-start.1
  7.1 1.2 collective-permute-start
  8.3 3.2 %collective-permute-start.5 = (bf16[16,256,256]{2,1,0:T(8,128)(2,1)}, bf16[16,256,256]{2,1,0:T(8,128)(2,1)}, u32[]{:S(2)}, u32[]{:S(2)}) collective-permute-start(bf16[16,256,256]{2,1,0:T(8,128)(2,1)} %get-tuple-element.50.rest_3_), channel_id=1, source_target_pairs={{0,8},{8,16},{16,24},{1,9},{9,17},{17,25},{2,10},{10,18},{18,26},{... | collective-permute-start | bytes 6291464 | tf_op jit(solution)/shard_map/ppermute | solution.py:789
  11.6 3.0 %collective-permute-start.6 = (bf16[16,256,256]{2,1,0:T(8,128)(2,1)}, bf16[16,256,256]{2,1,0:T(8,128)(2,1)}, u32[]{:S(2)}, u32[]{:S(2)}) collective-permute-start(bf16[16,256,256]{2,1,0:T(8,128)(2,1)} %get-tuple-element.51.rest_2_), channel_id=1, source_target_pairs={{8,0},{16,8},{24,16},{9,1},{17,9},{25,17},{10,2},{18,10},{26,18},{... | collective-permute-start | bytes 6291464 | tf_op jit(solution)/shard_map/ppermute | solution.py:790
  14.9 13.7 %near_first.1 = (f32[8,256,256]{2,1,0:T(8,128)}, bf16[22,256,256]{2,1,0:T(8,128)(2,1)}, s32[16,37]{1,0:T(8,128)}) custom-call(s32[4,4,9]{2,1,0:T(4,128)} %lists.3, s32[4,4,27]{2,1,0:T(4,128)} %far_zero.3, f32[512,2,256]{2,1,0:T(2,128)} %bitcast.15, bf16[16,256,256]{2,1,0:T(8,128)(2,1)} %bitcast.8), custom_call_target="tpu_custom_call" | custom-call | flops 50331648000 | bytes 1048576 | tf_op jit(solution)/shard_map/near_first/pallas_call | solution.py:375
  28.7 2.4 %pair_payload.1 = (bf16[8,256,256]{2,1,0:T(8,128)(2,1)}, bf16[4,256,256]{2,1,0:T(8,128)(2,1)}) custom-call(bf16[5,256,256]{2,1,0:T(8,128)(2,1)} %get-tuple-element.39.refs_0_.upper, bf16[5,256,256]{2,1,0:T(8,128)(2,1)} %collective-permute-done.refs_1_.refs_0_, bf16[1,256,256]{2,1,0:T(8,128)(2,1)} %copy-done, bf16[1,256,256]{2,1,0:T(8,128)(2,1)} %collective-permute-done.2.refs_3_), custom_call_target="tpu_custom_call" | custom-call | flops 146800640 | tf_op jit(solution)/shard_map/pair_payload/pallas_call | solution.py:185
  31.1 3.2 %collective-permute-start.8 = (bf16[8,256,256]{2,1,0:T(8,128)(2,1)}, bf16[8,256,256]{2,1,0:T(8,128)(2,1)}, u32[]{:S(2)}, u32[]{:S(2)}) collective-permute-start(bf16[8,256,256]{2,1,0:T(8,128)(2,1)} %get-tuple-element.53), channel_id=1, source_target_pairs={{0,2},{2,4},{4,6},{3,1},{5,3},{7,5},{8,10},{10,12},{12,14},{11,9},... | collective-permute-start | bytes 3145736 | tf_op jit(solution)/shard_map/ppermute | solution.py:811
  34.3 2.1 %collective-permute-start.7 = (bf16[4,256,256]{2,1,0:T(8,128)(2,1)}, bf16[4,256,256]{2,1,0:T(8,128)(2,1)}, u32[]{:S(2)}, u32[]{:S(2)}) collective-permute-start(bf16[4,256,256]{2,1,0:T(8,128)(2,1)} %get-tuple-element.52.cells), channel_id=1, source_target_pairs={{2,0},{4,2},{6,4},{1,3},{3,5},{5,7},{10,8},{12,10},{14,12},{9,11},... | collective-permute-start | bytes 1572872 | tf_op jit(solution)/shard_map/ppermute | solution.py:812
  36.7 4.1 %collective-permute-start.3 = (bf16[12,256,256]{2,1,0:T(8,128)(2,1)}, bf16[12,256,256]{2,1,0:T(8,128)(2,1)}, u32[]{:S(2)}, u32[]{:S(2)}) collective-permute-start(bf16[12,256,256]{2,1,0:T(8,128)(2,1)} %get-tuple-element.48), channel_id=1, source_target_pairs={{0,1},{1,2},{2,3},{3,4},{4,5},{5,6},{6,7},{8,9},{9,10},{10,11},{11... | collective-permute-start | bytes 4718600 | tf_op jit(solution)/shard_map/ppermute | solution.py:814
  40.8 2.1 %collective-permute-start.4 = (bf16[12,256,256]{2,1,0:T(8,128)(2,1)}, bf16[12,256,256]{2,1,0:T(8,128)(2,1)}, u32[]{:S(2)}, u32[]{:S(2)}) collective-permute-start(bf16[12,256,256]{2,1,0:T(8,128)(2,1)} %get-tuple-element.49), channel_id=1, source_target_pairs={{1,0},{2,1},{3,2},{4,3},{5,4},{6,5},{7,6},{9,8},{10,9},{11,10},{12... | collective-permute-start | bytes 4718600 | tf_op jit(solution)/shard_map/ppermute | solution.py:815
  42.9 19.9 %near_and_inner_far.1 = (f32[8,256,256]{2,1,0:T(8,128)}, bf16[22,256,256]{2,1,0:T(8,128)(2,1)}, f32[16,256,256]{2,1,0:T(8,128)}) custom-call(s32[4,4,9]{2,1,0:T(4,128)} %lists.3, s32[4,4,27]{2,1,0:T(4,128)} %far_zero.3, f32[512,2,256]{2,1,0:T(2,128)} %bitcast.16, bf16[16,256,256]{2,1,0:T(8,128)(2,1)} %bitcast.9, s32[16,37]{1,0:T(8,128)} %get-tuple-element.38.rest_0_.flags, ...), custom_call_target="tpu_custom_call" | custom-call | flops 2516582400 | bytes 1048576 | tf_op jit(solution)/shard_map/near_and_inner_far/pallas_call | solution.py:375
  62.8 2.9 %row_payload.1 = (bf16[8,256,256]{2,1,0:T(8,128)(2,1)}, bf16[8,256,256]{2,1,0:T(8,128)(2,1)}) custom-call(bf16[5,256,256]{2,1,0:T(8,128)(2,1)} %collective-permute-done.refs_1_.refs_0_, bf16[8,256,256]{2,1,0:T(8,128)(2,1)} %collective-permute-done.8.refs_1_, bf16[4,256,256]{2,1,0:T(8,128)(2,1)} %collective-permute-done.7.refs_2_), custom_call_target="tpu_custom_call" | custom-call | flops 146800640 | tf_op jit(solution)/shard_map/row_payload/pallas_call | solution.py:185
  66.7 3.5 %collective-permute-start.10 = (bf16[8,256,256]{2,1,0:T(8,128)(2,1)}, bf16[8,256,256]{2,1,0:T(8,128)(2,1)}, u32[]{:S(2)}, u32[]{:S(2)}) collective-permute-start(bf16[8,256,256]{2,1,0:T(8,128)(2,1)} %get-tuple-element.57.row), channel_id=1, source_target_pairs={{8,16},{16,8},{9,17},{17,9},{10,18},{18,10},{11,19},{19,11},{12,20... | collective-permute-start | bytes 3145736 | tf_op jit(solution)/shard_map/ppermute | solution.py:833
  70.2 13.2 %collective-permute-done.10.row_d = bf16[8,256,256]{2,1,0:T(8,128)(2,1)} collective-permute-done((bf16[8,256,256]{2,1,0:T(8,128)(2,1)}, bf16[8,256,256]{2,1,0:T(8,128)(2,1)}, u32[]{:S(2)}, u32[]{:S(2)}) %collective-permute-start.10) | collective-permute-done | bytes 1048608 | tf_op jit(solution)/shard_map/ppermute | solution.py:833
  83.4 10.7 %upper_levels.1.down_one = bf16[4,256,256]{2,1,0:T(8,128)(2,1)} custom-call(s32[2,2,27]{2,1,0:T(2,128)} %far_one.1, s32[1,1,27]{2,1,0:T(1,128)} %far_two.1, bf16[3,20,256,256]{3,2,1,0:T(8,128)(2,1)} %couplings.5, bf16[2,2,256,256]{3,2,1,0:T(8,128)(2,1)} %t_two.3, bf16[5,256,256]{2,1,0:T(8,128)(2,1)} %get-tuple-element.39.refs_0_.upper, ...), custom_call_target="tpu_custom_call" | custom-call | flops 1426063360 | bytes 1835008 | tf_op jit(solution)/shard_map/upper_levels/pallas_call | solution.py:511
  94.1 14.2 %collective-permute-done.3.left.refs_0_ = bf16[12,256,256]{2,1,0:T(8,128)(2,1)} collective-permute-done((bf16[12,256,256]{2,1,0:T(8,128)(2,1)}, bf16[12,256,256]{2,1,0:T(8,128)(2,1)}, u32[]{:S(2)}, u32[]{:S(2)}) %collective-permute-start.3) | collective-permute-done | bytes 1572896 | tf_op jit(solution)/shard_map/ppermute | solution.py:814
  108.3 3.8 %collective-permute-done.4.right.refs_1_ = bf16[12,256,256]{2,1,0:T(8,128)(2,1)} collective-permute-done((bf16[12,256,256]{2,1,0:T(8,128)(2,1)}, bf16[12,256,256]{2,1,0:T(8,128)(2,1)}, u32[]{:S(2)}, u32[]{:S(2)}) %collective-permute-start.4) | collective-permute-done | bytes 1572896 | tf_op jit(solution)/shard_map/ppermute | solution.py:815
  112.1 3.2 %corner_payload.1 = (bf16[10,256,256]{2,1,0:T(8,128)(2,1)}, bf16[10,256,256]{2,1,0:T(8,128)(2,1)}) custom-call(bf16[12,256,256]{2,1,0:T(8,128)(2,1)} %collective-permute-done.3.left.refs_0_, bf16[12,256,256]{2,1,0:T(8,128)(2,1)} %collective-permute-done.4.right.refs_1_), custom_call_target="tpu_custom_call" | custom-call | flops 146800640 | tf_op jit(solution)/shard_map/corner_payload/pallas_call | solution.py:185
  115.3 5.1 %collective-permute-start.13 = (bf16[10,256,256]{2,1,0:T(8,128)(2,1)}, bf16[10,256,256]{2,1,0:T(8,128)(2,1)}, u32[]{:S(2)}, u32[]{:S(2)}) collective-permute-start(bf16[10,256,256]{2,1,0:T(8,128)(2,1)} %get-tuple-element.69), channel_id=1, source_target_pairs={{0,8},{8,16},{16,24},{1,9},{9,17},{17,25},{2,10},{10,18},{18,26},{... | collective-permute-start | bytes 3932168 | tf_op jit(solution)/shard_map/ppermute | solution.py:850
  120.4 1.9 %collective-permute-start.14 = (bf16[10,256,256]{2,1,0:T(8,128)(2,1)}, bf16[10,256,256]{2,1,0:T(8,128)(2,1)}, u32[]{:S(2)}, u32[]{:S(2)}) collective-permute-start(bf16[10,256,256]{2,1,0:T(8,128)(2,1)} %get-tuple-element.70), channel_id=1, source_target_pairs={{8,0},{16,8},{24,16},{9,1},{17,9},{25,17},{10,2},{18,10},{26,18},{... | collective-permute-start | bytes 3932168 | tf_op jit(solution)/shard_map/ppermute | solution.py:851
  122.3 14.2 %far_sides.1 = (f32[2,2,2,2,256,256]{5,4,3,2,1,0:T(8,128)}, f32[2,2,2,2,256,256]{5,4,3,2,1,0:T(8,128)}) custom-call(s32[16,37]{1,0:T(8,128)} %get-tuple-element.38.rest_0_.flags, bf16[3,20,256,256]{3,2,1,0:T(8,128)(2,1)} %couplings.5, f32[2,2,2,2,256,256]{5,4,3,2,1,0:T(8,128)} %bitcast.12, f32[2,2,2,256,256]{4,3,2,1,0:T(8,128)} %bitcast.13, ...), custom_call_target="tpu_custom_call" | custom-call | flops 1258291200 | bytes 3932160 | tf_op jit(solution)/shard_map/far_sides/pallas_call | solution.py:669
  136.5 3.1 %collective-permute-done.14.below = bf16[10,256,256]{2,1,0:T(8,128)(2,1)} collective-permute-done((bf16[10,256,256]{2,1,0:T(8,128)(2,1)}, bf16[10,256,256]{2,1,0:T(8,128)(2,1)}, u32[]{:S(2)}, u32[]{:S(2)}) %collective-permute-start.14) | collective-permute-done | bytes 1310752 | tf_op jit(solution)/shard_map/ppermute | solution.py:851
  139.6 12.7 %last_level.1 = bf16[2,2,2,2,256,256]{5,4,3,2,1,0:T(8,128)(2,1)} custom-call(s32[16,37]{1,0:T(8,128)} %get-tuple-element.38.rest_0_.flags, bf16[3,20,256,256]{3,2,1,0:T(8,128)(2,1)} %couplings.5, bf16[2,2,2,2,256,256]{5,4,3,2,1,0:T(8,128)(2,1)} %bitcast.10, bf16[2,2,2,2,256,256]{5,4,3,2,1,0:T(8,128)(2,1)} %bitcast.11, ...), custom_call_target="tpu_custom_call" | custom-call | flops 1132462080 | bytes 2621440 | tf_op jit(solution)/shard_map/last_level/pallas_call | solution.py:727
  (17 shorter events, 1.6 us)
Async XLA Ops:
  5.8 8.8 %collective-permute-start.1 = (bf16[1,256,256]{2,1,0:T(8,128)(2,1)}, bf16[1,256,256]{2,1,0:T(8,128)(2,1)S(1)}, u32[]{:S(2)}, u32[]{:S(2)}) collective-permute-start(bf16[1,256,256]{2,1,0:T(8,128)(2,1)} %get-tuple-element.40), channel_id=1, source_target_pairs={{0,16},{8,24},{16,0},{24,8},{1,17},{9,25},{17,1},{25,9},{2,18},{10... | collective-permute-start | bytes 393224 | tf_op jit(solution)/shard_map/ppermute | solution.py:782
  7.1 21.5 %collective-permute-start = (bf16[5,256,256]{2,1,0:T(8,128)(2,1)}, bf16[5,256,256]{2,1,0:T(8,128)(2,1)}, u32[]{:S(2)}, u32[]{:S(2)}) collective-permute-start(bf16[5,256,256]{2,1,0:T(8,128)(2,1)} %get-tuple-element.39.refs_0_.upper), channel_id=1, source_target_pairs={{0,1},{1,0},{2,3},{3,2},{4,5},{5,4},{6,7},{7,6},{8,9},{9,8},{10,11... | collective-permute-start | bytes 1966088 | tf_op jit(solution)/shard_map/ppermute | solution.py:780
  8.3 28.4 %collective-permute-start.5 = (bf16[16,256,256]{2,1,0:T(8,128)(2,1)}, bf16[16,256,256]{2,1,0:T(8,128)(2,1)}, u32[]{:S(2)}, u32[]{:S(2)}) collective-permute-start(bf16[16,256,256]{2,1,0:T(8,128)(2,1)} %get-tuple-element.50.rest_3_), channel_id=1, source_target_pairs={{0,8},{8,16},{16,24},{1,9},{9,17},{17,25},{2,10},{10,18},{18,26},{... | collective-permute-start | bytes 6291464 | tf_op jit(solution)/shard_map/ppermute | solution.py:789
  11.6 29.2 %collective-permute-start.6 = (bf16[16,256,256]{2,1,0:T(8,128)(2,1)}, bf16[16,256,256]{2,1,0:T(8,128)(2,1)}, u32[]{:S(2)}, u32[]{:S(2)}) collective-permute-start(bf16[16,256,256]{2,1,0:T(8,128)(2,1)} %get-tuple-element.51.rest_2_), channel_id=1, source_target_pairs={{8,0},{16,8},{24,16},{9,1},{17,9},{25,17},{10,2},{18,10},{26,18},{... | collective-permute-start | bytes 6291464 | tf_op jit(solution)/shard_map/ppermute | solution.py:790
  14.6 14.0 %copy-start = (bf16[1,256,256]{2,1,0:T(8,128)(2,1)}, bf16[1,256,256]{2,1,0:T(8,128)(2,1)S(1)}, u32[]{:S(2)}) copy-start(bf16[1,256,256]{2,1,0:T(8,128)(2,1)S(1)} %collective-permute-done.1.refs_2_) | copy-start | bytes 393220
  14.6 14.0 %collective-permute-start.2 = (bf16[1,256,256]{2,1,0:T(8,128)(2,1)S(1)}, bf16[1,256,256]{2,1,0:T(8,128)(2,1)}, u32[]{:S(2)}, u32[]{:S(2)}) collective-permute-start(bf16[1,256,256]{2,1,0:T(8,128)(2,1)S(1)} %collective-permute-done.1.refs_2_), channel_id=1, source_target_pairs={{0,1},{1,0},{2,3},{3,2},{4,5},{5,4},{6,7},{7,6},{8,9},{9,8},{10,11... | collective-permute-start | bytes 393224 | tf_op jit(solution)/shard_map/ppermute | solution.py:788
  31.1 31.7 %collective-permute-start.8 = (bf16[8,256,256]{2,1,0:T(8,128)(2,1)}, bf16[8,256,256]{2,1,0:T(8,128)(2,1)}, u32[]{:S(2)}, u32[]{:S(2)}) collective-permute-start(bf16[8,256,256]{2,1,0:T(8,128)(2,1)} %get-tuple-element.53), channel_id=1, source_target_pairs={{0,2},{2,4},{4,6},{3,1},{5,3},{7,5},{8,10},{10,12},{12,14},{11,9},... | collective-permute-start | bytes 3145736 | tf_op jit(solution)/shard_map/ppermute | solution.py:811
  34.3 28.5 %collective-permute-start.7 = (bf16[4,256,256]{2,1,0:T(8,128)(2,1)}, bf16[4,256,256]{2,1,0:T(8,128)(2,1)}, u32[]{:S(2)}, u32[]{:S(2)}) collective-permute-start(bf16[4,256,256]{2,1,0:T(8,128)(2,1)} %get-tuple-element.52.cells), channel_id=1, source_target_pairs={{2,0},{4,2},{6,4},{1,3},{3,5},{5,7},{10,8},{12,10},{14,12},{9,11},... | collective-permute-start | bytes 1572872 | tf_op jit(solution)/shard_map/ppermute | solution.py:812
  36.4 33.7 %collective-permute-start.11 = (bf16[4,256,256]{2,1,0:T(8,128)(2,1)}, bf16[4,256,256]{2,1,0:T(8,128)(2,1)}, u32[]{:S(2)}, u32[]{:S(2)}) collective-permute-start(bf16[4,256,256]{2,1,0:T(8,128)(2,1)} %get-tuple-element.52.cells), channel_id=1, source_target_pairs={{0,8},{8,0},{16,24},{24,16},{1,9},{9,1},{17,25},{25,17},{2,10},{10... | collective-permute-start | bytes 1572872 | tf_op jit(solution)/shard_map/ppermute | solution.py:813
  36.7 71.6 %collective-permute-start.3 = (bf16[12,256,256]{2,1,0:T(8,128)(2,1)}, bf16[12,256,256]{2,1,0:T(8,128)(2,1)}, u32[]{:S(2)}, u32[]{:S(2)}) collective-permute-start(bf16[12,256,256]{2,1,0:T(8,128)(2,1)} %get-tuple-element.48), channel_id=1, source_target_pairs={{0,1},{1,2},{2,3},{3,4},{4,5},{5,6},{6,7},{8,9},{9,10},{10,11},{11... | collective-permute-start | bytes 4718600 | tf_op jit(solution)/shard_map/ppermute | solution.py:814
  40.8 71.3 %collective-permute-start.4 = (bf16[12,256,256]{2,1,0:T(8,128)(2,1)}, bf16[12,256,256]{2,1,0:T(8,128)(2,1)}, u32[]{:S(2)}, u32[]{:S(2)}) collective-permute-start(bf16[12,256,256]{2,1,0:T(8,128)(2,1)} %get-tuple-element.49), channel_id=1, source_target_pairs={{1,0},{2,1},{3,2},{4,3},{5,4},{6,5},{7,6},{9,8},{10,9},{11,10},{12... | collective-permute-start | bytes 4718600 | tf_op jit(solution)/shard_map/ppermute | solution.py:815
  65.7 4.5 %collective-permute-start.9 = (bf16[8,256,256]{2,1,0:T(8,128)(2,1)}, bf16[8,256,256]{2,1,0:T(8,128)(2,1)}, u32[]{:S(2)}, u32[]{:S(2)}) collective-permute-start(bf16[8,256,256]{2,1,0:T(8,128)(2,1)} %get-tuple-element.57.row), channel_id=1, source_target_pairs={{0,8},{8,0},{16,24},{24,16},{1,9},{9,1},{17,25},{25,17},{2,10},{10... | collective-permute-start | bytes 3145736 | tf_op jit(solution)/shard_map/ppermute | solution.py:834
  66.7 16.7 %collective-permute-start.10 = (bf16[8,256,256]{2,1,0:T(8,128)(2,1)}, bf16[8,256,256]{2,1,0:T(8,128)(2,1)}, u32[]{:S(2)}, u32[]{:S(2)}) collective-permute-start(bf16[8,256,256]{2,1,0:T(8,128)(2,1)} %get-tuple-element.57.row), channel_id=1, source_target_pairs={{8,16},{16,8},{9,17},{17,9},{10,18},{18,10},{11,19},{19,11},{12,20... | collective-permute-start | bytes 3145736 | tf_op jit(solution)/shard_map/ppermute | solution.py:833
  70.1 13.2 %collective-permute-start.12 = (bf16[8,256,256]{2,1,0:T(8,128)(2,1)}, bf16[8,256,256]{2,1,0:T(8,128)(2,1)}, u32[]{:S(2)}, u32[]{:S(2)}) collective-permute-start(bf16[8,256,256]{2,1,0:T(8,128)(2,1)} %get-tuple-element.58.quads), channel_id=1, source_target_pairs={{0,8},{8,0},{16,24},{24,16},{1,9},{9,1},{17,25},{25,17},{2,10},{10... | collective-permute-start | bytes 3145736 | tf_op jit(solution)/shard_map/ppermute | solution.py:835
  115.3 21.3 %collective-permute-start.13 = (bf16[10,256,256]{2,1,0:T(8,128)(2,1)}, bf16[10,256,256]{2,1,0:T(8,128)(2,1)}, u32[]{:S(2)}, u32[]{:S(2)}) collective-permute-start(bf16[10,256,256]{2,1,0:T(8,128)(2,1)} %get-tuple-element.69), channel_id=1, source_target_pairs={{0,8},{8,16},{16,24},{1,9},{9,17},{17,25},{2,10},{10,18},{18,26},{... | collective-permute-start | bytes 3932168 | tf_op jit(solution)/shard_map/ppermute | solution.py:850
  120.4 19.2 %collective-permute-start.14 = (bf16[10,256,256]{2,1,0:T(8,128)(2,1)}, bf16[10,256,256]{2,1,0:T(8,128)(2,1)}, u32[]{:S(2)}, u32[]{:S(2)}) collective-permute-start(bf16[10,256,256]{2,1,0:T(8,128)(2,1)} %get-tuple-element.70), channel_id=1, source_target_pairs={{8,0},{16,8},{24,16},{9,1},{17,9},{25,17},{10,2},{18,10},{26,18},{... | collective-permute-start | bytes 3932168 | tf_op jit(solution)/shard_map/ppermute | solution.py:851

commit v2 on v1

--- a/solution.py
+++ b/solution.py
@@ -75,6 +75,12 @@
 ANY_SPEC = pl.BlockSpec(memory_space=pltpu.HBM)
 SMEM_SPEC = pl.BlockSpec(memory_space=SMEM)
 VMEM_SPEC = pl.BlockSpec(memory_space=VMEM)
+
+
+def row_number(entry, grid_cols):
+    if grid_cols & (grid_cols - 1) == 0:
+        return entry >> (grid_cols.bit_length() - 1)
+    return lax.div(entry, jnp.int32(grid_cols))
 
 
 class Copies:
@@ -304,7 +310,7 @@
             floors[m * 10 + k] = 1e6
         for e in range(9):
             entry = lists[r, c, e]
-            source_row = jnp.maximum(entry, 0) // grid_cols
+            source_row = row_number(jnp.maximum(entry, 0), grid_cols)
             source_col = jnp.maximum(entry, 0) - source_row * grid_cols
             k = (source_row - first_row - r + 1) * 3 + source_col - first_col - c + 1
             floors[m * 10 + jnp.where(entry >= 0, k, 9)] = 1e-24
@@ -402,7 +408,7 @@
         flags[n, w] = 0
     for e in range(27):
         entry = entries(e)
-        row = jnp.maximum(entry, 0) // grid_cols
+        row = row_number(jnp.maximum(entry, 0), grid_cols)
         col = jnp.maximum(entry, 0) - row * grid_cols
         w = (row - first_row) * 6 + col - first_col
         flags[n, jnp.where(entry >= 0, jnp.clip(w, 0, 35), 36)] = 1

time: 156 us -> 155 us (level)
  no operation moved by 1% of the time
where the time goes in v2:
time: 155 us; the launch traced here: 152 us
  Pallas kernels  84.8 us (55%)
  waiting for transfers between devices  34.3 us (22%)
  starting transfers between devices  32.3 us (21%)
    pallas_call x2, Pallas kernels, near_call(): pl.pallas_call(functools.partial(near_kernel, first, bool(far), grid_rows...  32.9 us
    pallas_call x1, Pallas kernels, sides_level(): pl.pallas_call(sides_kernel, grid=(4,), out_shape=(GROUPED_F32, GROUPED_F...  14.2 us
    ppermute x1, waiting for transfers between devices, per_device(): on_left = lax.ppermute(right, 'qy', down_y)  14.2 us
    ppermute x1, waiting for transfers between devices, per_device(): row_d = lax.ppermute(row, 'qx', cross_x)  13.1 us
    pallas_call x1, Pallas kernels, last_level(): pl.pallas_call(last_kernel, grid=(4,), out_shape=jax.ShapeDtypeStruct((2,...  12.7 us
    pallas_call x1, Pallas kernels, upper_levels(): pl.pallas_call(functools.partial(upper_kernel, grid_cols, n_two // 6), gr...  10.7 us
    pallas_call x3, Pallas kernels, assembled(): pl.pallas_call(kernel, out_shape=[tiles(last - first) for first, last in...  8.49 us
    pallas_call x1, Pallas kernels, coefficients(): pl.pallas_call(coef_kernel, out_shape=[tiles(n) for n in (16, 16, 12, 12,...  5.8 us
  transfers between devices with their start and end apart: 15, of which 4 were waited for; matrix products, arithmetic and copies ran while one was open for 0% of the time, Pallas kernels for 42%

profile of v2, /device:TPU:17, one launch (start us, length us, event | category | flops | bytes accessed | tf_op | source)
XLA Modules:
  0.0 151.9 jit_solution(93483646970822118)
XLA Ops:
  0.0 5.8 %coefficients.1 = (bf16[16,256,256]{2,1,0:T(8,128)(2,1)}, bf16[16,256,256]{2,1,0:T(8,128)(2,1)}, bf16[12,256,256]{2,1,0:T(8,128)(2,1)}, bf16[12,256,256]{2,1,0:T...) custom-call(bf16[4,4,256,256]{3,2,1,0:T(8,128)(2,1)} %samples.1, ...), custom_call_target="tpu_custom_call" | custom-call | flops 713031680 | bytes 1572864 | tf_op jit(solution)/shard_map/coefficients/pallas_call | solution.py:153
  5.8 1.3 collective-permute-start.1
  7.1 1.2 collective-permute-start
  8.3 3.2 %collective-permute-start.5 = (bf16[16,256,256]{2,1,0:T(8,128)(2,1)}, bf16[16,256,256]{2,1,0:T(8,128)(2,1)}, u32[]{:S(2)}, u32[]{:S(2)}) collective-permute-start(bf16[16,256,256]{2,1,0:T(8,128)(2,1)} %get-tuple-element.50.rest_3_), channel_id=1, source_target_pairs={{0,8},{8,16},{16,24},{1,9},{9,17},{17,25},{2,10},{10,18},{18,26},{... | collective-permute-start | bytes 6291464 | tf_op jit(solution)/shard_map/ppermute | solution.py:795
  11.6 3.0 %collective-permute-start.6 = (bf16[16,256,256]{2,1,0:T(8,128)(2,1)}, bf16[16,256,256]{2,1,0:T(8,128)(2,1)}, u32[]{:S(2)}, u32[]{:S(2)}) collective-permute-start(bf16[16,256,256]{2,1,0:T(8,128)(2,1)} %get-tuple-element.51.rest_2_), channel_id=1, source_target_pairs={{8,0},{16,8},{24,16},{9,1},{17,9},{25,17},{10,2},{18,10},{26,18},{... | collective-permute-start | bytes 6291464 | tf_op jit(solution)/shard_map/ppermute | solution.py:796
  14.9 13.0 %near_first.1 = (f32[8,256,256]{2,1,0:T(8,128)}, bf16[22,256,256]{2,1,0:T(8,128)(2,1)}, s32[16,37]{1,0:T(8,128)}) custom-call(s32[4,4,9]{2,1,0:T(4,128)} %lists.3, s32[4,4,27]{2,1,0:T(4,128)} %far_zero.3, f32[512,2,256]{2,1,0:T(2,128)} %bitcast.15, bf16[16,256,256]{2,1,0:T(8,128)(2,1)} %bitcast.8), custom_call_target="tpu_custom_call" | custom-call | flops 50331648000 | bytes 1048576 | tf_op jit(solution)/shard_map/near_first/pallas_call | solution.py:381
  27.9 2.4 %pair_payload.1 = (bf16[8,256,256]{2,1,0:T(8,128)(2,1)}, bf16[4,256,256]{2,1,0:T(8,128)(2,1)}) custom-call(bf16[5,256,256]{2,1,0:T(8,128)(2,1)} %get-tuple-element.39.refs_0_.upper, bf16[5,256,256]{2,1,0:T(8,128)(2,1)} %collective-permute-done.refs_1_.refs_0_, bf16[1,256,256]{2,1,0:T(8,128)(2,1)} %copy-done, bf16[1,256,256]{2,1,0:T(8,128)(2,1)} %collective-permute-done.2.refs_3_), custom_call_target="tpu_custom_call" | custom-call | flops 146800640 | tf_op jit(solution)/shard_map/pair_payload/pallas_call | solution.py:191
  30.4 3.2 %collective-permute-start.8 = (bf16[8,256,256]{2,1,0:T(8,128)(2,1)}, bf16[8,256,256]{2,1,0:T(8,128)(2,1)}, u32[]{:S(2)}, u32[]{:S(2)}) collective-permute-start(bf16[8,256,256]{2,1,0:T(8,128)(2,1)} %get-tuple-element.53), channel_id=1, source_target_pairs={{0,2},{2,4},{4,6},{3,1},{5,3},{7,5},{8,10},{10,12},{12,14},{11,9},... | collective-permute-start | bytes 3145736 | tf_op jit(solution)/shard_map/ppermute | solution.py:817
  33.6 2.1 %collective-permute-start.7 = (bf16[4,256,256]{2,1,0:T(8,128)(2,1)}, bf16[4,256,256]{2,1,0:T(8,128)(2,1)}, u32[]{:S(2)}, u32[]{:S(2)}) collective-permute-start(bf16[4,256,256]{2,1,0:T(8,128)(2,1)} %get-tuple-element.52.cells), channel_id=1, source_target_pairs={{2,0},{4,2},{6,4},{1,3},{3,5},{5,7},{10,8},{12,10},{14,12},{9,11},... | collective-permute-start | bytes 1572872 | tf_op jit(solution)/shard_map/ppermute | solution.py:818
  36.0 4.1 %collective-permute-start.3 = (bf16[12,256,256]{2,1,0:T(8,128)(2,1)}, bf16[12,256,256]{2,1,0:T(8,128)(2,1)}, u32[]{:S(2)}, u32[]{:S(2)}) collective-permute-start(bf16[12,256,256]{2,1,0:T(8,128)(2,1)} %get-tuple-element.48), channel_id=1, source_target_pairs={{0,1},{1,2},{2,3},{3,4},{4,5},{5,6},{6,7},{8,9},{9,10},{10,11},{11... | collective-permute-start | bytes 4718600 | tf_op jit(solution)/shard_map/ppermute | solution.py:820
  40.0 2.1 %collective-permute-start.4 = (bf16[12,256,256]{2,1,0:T(8,128)(2,1)}, bf16[12,256,256]{2,1,0:T(8,128)(2,1)}, u32[]{:S(2)}, u32[]{:S(2)}) collective-permute-start(bf16[12,256,256]{2,1,0:T(8,128)(2,1)} %get-tuple-element.49), channel_id=1, source_target_pairs={{1,0},{2,1},{3,2},{4,3},{5,4},{6,5},{7,6},{9,8},{10,9},{11,10},{12... | collective-permute-start | bytes 4718600 | tf_op jit(solution)/shard_map/ppermute | solution.py:821
  42.2 19.9 %near_and_inner_far.1 = (f32[8,256,256]{2,1,0:T(8,128)}, bf16[22,256,256]{2,1,0:T(8,128)(2,1)}, f32[16,256,256]{2,1,0:T(8,128)}) custom-call(s32[4,4,9]{2,1,0:T(4,128)} %lists.3, s32[4,4,27]{2,1,0:T(4,128)} %far_zero.3, f32[512,2,256]{2,1,0:T(2,128)} %bitcast.16, bf16[16,256,256]{2,1,0:T(8,128)(2,1)} %bitcast.9, s32[16,37]{1,0:T(8,128)} %get-tuple-element.38.rest_0_.flags, ...), custom_call_target="tpu_custom_call" | custom-call | flops 2516582400 | bytes 1048576 | tf_op jit(solution)/shard_map/near_and_inner_far/pallas_call | solution.py:381
  62.1 2.9 %row_payload.1 = (bf16[8,256,256]{2,1,0:T(8,128)(2,1)}, bf16[8,256,256]{2,1,0:T(8,128)(2,1)}) custom-call(bf16[5,256,256]{2,1,0:T(8,128)(2,1)} %collective-permute-done.refs_1_.refs_0_, bf16[8,256,256]{2,1,0:T(8,128)(2,1)} %collective-permute-done.8.refs_1_, bf16[4,256,256]{2,1,0:T(8,128)(2,1)} %collective-permute-done.7.refs_2_), custom_call_target="tpu_custom_call" | custom-call | flops 146800640 | tf_op jit(solution)/shard_map/row_payload/pallas_call | solution.py:191
  65.9 3.5 %collective-permute-start.10 = (bf16[8,256,256]{2,1,0:T(8,128)(2,1)}, bf16[8,256,256]{2,1,0:T(8,128)(2,1)}, u32[]{:S(2)}, u32[]{:S(2)}) collective-permute-start(bf16[8,256,256]{2,1,0:T(8,128)(2,1)} %get-tuple-element.57.row), channel_id=1, source_target_pairs={{8,16},{16,8},{9,17},{17,9},{10,18},{18,10},{11,19},{19,11},{12,20... | collective-permute-start | bytes 3145736 | tf_op jit(solution)/shard_map/ppermute | solution.py:839
  69.5 13.1 %collective-permute-done.10.row_d = bf16[8,256,256]{2,1,0:T(8,128)(2,1)} collective-permute-done((bf16[8,256,256]{2,1,0:T(8,128)(2,1)}, bf16[8,256,256]{2,1,0:T(8,128)(2,1)}, u32[]{:S(2)}, u32[]{:S(2)}) %collective-permute-start.10) | collective-permute-done | bytes 1048608 | tf_op jit(solution)/shard_map/ppermute | solution.py:839
  82.6 10.7 %upper_levels.1.down_one = bf16[4,256,256]{2,1,0:T(8,128)(2,1)} custom-call(s32[2,2,27]{2,1,0:T(2,128)} %far_one.1, s32[1,1,27]{2,1,0:T(1,128)} %far_two.1, bf16[3,20,256,256]{3,2,1,0:T(8,128)(2,1)} %couplings.5, bf16[2,2,256,256]{3,2,1,0:T(8,128)(2,1)} %t_two.3, bf16[5,256,256]{2,1,0:T(8,128)(2,1)} %get-tuple-element.39.refs_0_.upper, ...), custom_call_target="tpu_custom_call" | custom-call | flops 1426063360 | bytes 1835008 | tf_op jit(solution)/shard_map/upper_levels/pallas_call | solution.py:517
  93.3 14.2 %collective-permute-done.3.left.refs_0_ = bf16[12,256,256]{2,1,0:T(8,128)(2,1)} collective-permute-done((bf16[12,256,256]{2,1,0:T(8,128)(2,1)}, bf16[12,256,256]{2,1,0:T(8,128)(2,1)}, u32[]{:S(2)}, u32[]{:S(2)}) %collective-permute-start.3) | collective-permute-done | bytes 1572896 | tf_op jit(solution)/shard_map/ppermute | solution.py:820
  107.5 3.8 %collective-permute-done.4.right.refs_1_ = bf16[12,256,256]{2,1,0:T(8,128)(2,1)} collective-permute-done((bf16[12,256,256]{2,1,0:T(8,128)(2,1)}, bf16[12,256,256]{2,1,0:T(8,128)(2,1)}, u32[]{:S(2)}, u32[]{:S(2)}) %collective-permute-start.4) | collective-permute-done | bytes 1572896 | tf_op jit(solution)/shard_map/ppermute | solution.py:821
  111.3 3.2 %corner_payload.1 = (bf16[10,256,256]{2,1,0:T(8,128)(2,1)}, bf16[10,256,256]{2,1,0:T(8,128)(2,1)}) custom-call(bf16[12,256,256]{2,1,0:T(8,128)(2,1)} %collective-permute-done.3.left.refs_0_, bf16[12,256,256]{2,1,0:T(8,128)(2,1)} %collective-permute-done.4.right.refs_1_), custom_call_target="tpu_custom_call" | custom-call | flops 146800640 | tf_op jit(solution)/shard_map/corner_payload/pallas_call | solution.py:191
  114.5 5.1 %collective-permute-start.13 = (bf16[10,256,256]{2,1,0:T(8,128)(2,1)}, bf16[10,256,256]{2,1,0:T(8,128)(2,1)}, u32[]{:S(2)}, u32[]{:S(2)}) collective-permute-start(bf16[10,256,256]{2,1,0:T(8,128)(2,1)} %get-tuple-element.69), channel_id=1, source_target_pairs={{0,8},{8,16},{16,24},{1,9},{9,17},{17,25},{2,10},{10,18},{18,26},{... | collective-permute-start | bytes 3932168 | tf_op jit(solution)/shard_map/ppermute | solution.py:856
  119.7 1.9 %collective-permute-start.14 = (bf16[10,256,256]{2,1,0:T(8,128)(2,1)}, bf16[10,256,256]{2,1,0:T(8,128)(2,1)}, u32[]{:S(2)}, u32[]{:S(2)}) collective-permute-start(bf16[10,256,256]{2,1,0:T(8,128)(2,1)} %get-tuple-element.70), channel_id=1, source_target_pairs={{8,0},{16,8},{24,16},{9,1},{17,9},{25,17},{10,2},{18,10},{26,18},{... | collective-permute-start | bytes 3932168 | tf_op jit(solution)/shard_map/ppermute | solution.py:857
  121.6 14.2 %far_sides.1 = (f32[2,2,2,2,256,256]{5,4,3,2,1,0:T(8,128)}, f32[2,2,2,2,256,256]{5,4,3,2,1,0:T(8,128)}) custom-call(s32[16,37]{1,0:T(8,128)} %get-tuple-element.38.rest_0_.flags, bf16[3,20,256,256]{3,2,1,0:T(8,128)(2,1)} %couplings.5, f32[2,2,2,2,256,256]{5,4,3,2,1,0:T(8,128)} %bitcast.12, f32[2,2,2,256,256]{4,3,2,1,0:T(8,128)} %bitcast.13, ...), custom_call_target="tpu_custom_call" | custom-call | flops 1258291200 | bytes 3932160 | tf_op jit(solution)/shard_map/far_sides/pallas_call | solution.py:675
  135.8 3.1 %collective-permute-done.14.below = bf16[10,256,256]{2,1,0:T(8,128)(2,1)} collective-permute-done((bf16[10,256,256]{2,1,0:T(8,128)(2,1)}, bf16[10,256,256]{2,1,0:T(8,128)(2,1)}, u32[]{:S(2)}, u32[]{:S(2)}) %collective-permute-start.14) | collective-permute-done | bytes 1310752 | tf_op jit(solution)/shard_map/ppermute | solution.py:857
  138.9 12.7 %last_level.1 = bf16[2,2,2,2,256,256]{5,4,3,2,1,0:T(8,128)(2,1)} custom-call(s32[16,37]{1,0:T(8,128)} %get-tuple-element.38.rest_0_.flags, bf16[3,20,256,256]{3,2,1,0:T(8,128)(2,1)} %couplings.5, bf16[2,2,2,2,256,256]{5,4,3,2,1,0:T(8,128)(2,1)} %bitcast.10, bf16[2,2,2,2,256,256]{5,4,3,2,1,0:T(8,128)(2,1)} %bitcast.11, ...), custom_call_target="tpu_custom_call" | custom-call | flops 1132462080 | bytes 2621440 | tf_op jit(solution)/shard_map/last_level/pallas_call | solution.py:733
  (17 shorter events, 1.6 us)
Async XLA Ops:
  5.8 8.8 %collective-permute-start.1 = (bf16[1,256,256]{2,1,0:T(8,128)(2,1)}, bf16[1,256,256]{2,1,0:T(8,128)(2,1)S(1)}, u32[]{:S(2)}, u32[]{:S(2)}) collective-permute-start(bf16[1,256,256]{2,1,0:T(8,128)(2,1)} %get-tuple-element.40), channel_id=1, source_target_pairs={{0,16},{8,24},{16,0},{24,8},{1,17},{9,25},{17,1},{25,9},{2,18},{10... | collective-permute-start | bytes 393224 | tf_op jit(solution)/shard_map/ppermute | solution.py:788
  7.1 20.8 %collective-permute-start = (bf16[5,256,256]{2,1,0:T(8,128)(2,1)}, bf16[5,256,256]{2,1,0:T(8,128)(2,1)}, u32[]{:S(2)}, u32[]{:S(2)}) collective-permute-start(bf16[5,256,256]{2,1,0:T(8,128)(2,1)} %get-tuple-element.39.refs_0_.upper), channel_id=1, source_target_pairs={{0,1},{1,0},{2,3},{3,2},{4,5},{5,4},{6,7},{7,6},{8,9},{9,8},{10,11... | collective-permute-start | bytes 1966088 | tf_op jit(solution)/shard_map/ppermute | solution.py:786
  8.3 27.6 %collective-permute-start.5 = (bf16[16,256,256]{2,1,0:T(8,128)(2,1)}, bf16[16,256,256]{2,1,0:T(8,128)(2,1)}, u32[]{:S(2)}, u32[]{:S(2)}) collective-permute-start(bf16[16,256,256]{2,1,0:T(8,128)(2,1)} %get-tuple-element.50.rest_3_), channel_id=1, source_target_pairs={{0,8},{8,16},{16,24},{1,9},{9,17},{17,25},{2,10},{10,18},{18,26},{... | collective-permute-start | bytes 6291464 | tf_op jit(solution)/shard_map/ppermute | solution.py:795
  11.6 28.4 %collective-permute-start.6 = (bf16[16,256,256]{2,1,0:T(8,128)(2,1)}, bf16[16,256,256]{2,1,0:T(8,128)(2,1)}, u32[]{:S(2)}, u32[]{:S(2)}) collective-permute-start(bf16[16,256,256]{2,1,0:T(8,128)(2,1)} %get-tuple-element.51.rest_2_), channel_id=1, source_target_pairs={{8,0},{16,8},{24,16},{9,1},{17,9},{25,17},{10,2},{18,10},{26,18},{... | collective-permute-start | bytes 6291464 | tf_op jit(solution)/shard_map/ppermute | solution.py:796
  14.6 13.3 %copy-start = (bf16[1,256,256]{2,1,0:T(8,128)(2,1)}, bf16[1,256,256]{2,1,0:T(8,128)(2,1)S(1)}, u32[]{:S(2)}) copy-start(bf16[1,256,256]{2,1,0:T(8,128)(2,1)S(1)} %collective-permute-done.1.refs_2_) | copy-start | bytes 393220
  14.6 13.3 %collective-permute-start.2 = (bf16[1,256,256]{2,1,0:T(8,128)(2,1)S(1)}, bf16[1,256,256]{2,1,0:T(8,128)(2,1)}, u32[]{:S(2)}, u32[]{:S(2)}) collective-permute-start(bf16[1,256,256]{2,1,0:T(8,128)(2,1)S(1)} %collective-permute-done.1.refs_2_), channel_id=1, source_target_pairs={{0,1},{1,0},{2,3},{3,2},{4,5},{5,4},{6,7},{7,6},{8,9},{9,8},{10,11... | collective-permute-start | bytes 393224 | tf_op jit(solution)/shard_map/ppermute | solution.py:794
  30.4 31.7 %collective-permute-start.8 = (bf16[8,256,256]{2,1,0:T(8,128)(2,1)}, bf16[8,256,256]{2,1,0:T(8,128)(2,1)}, u32[]{:S(2)}, u32[]{:S(2)}) collective-permute-start(bf16[8,256,256]{2,1,0:T(8,128)(2,1)} %get-tuple-element.53), channel_id=1, source_target_pairs={{0,2},{2,4},{4,6},{3,1},{5,3},{7,5},{8,10},{10,12},{12,14},{11,9},... | collective-permute-start | bytes 3145736 | tf_op jit(solution)/shard_map/ppermute | solution.py:817
  33.6 28.5 %collective-permute-start.7 = (bf16[4,256,256]{2,1,0:T(8,128)(2,1)}, bf16[4,256,256]{2,1,0:T(8,128)(2,1)}, u32[]{:S(2)}, u32[]{:S(2)}) collective-permute-start(bf16[4,256,256]{2,1,0:T(8,128)(2,1)} %get-tuple-element.52.cells), channel_id=1, source_target_pairs={{2,0},{4,2},{6,4},{1,3},{3,5},{5,7},{10,8},{12,10},{14,12},{9,11},... | collective-permute-start | bytes 1572872 | tf_op jit(solution)/shard_map/ppermute | solution.py:818
  35.7 33.7 %collective-permute-start.11 = (bf16[4,256,256]{2,1,0:T(8,128)(2,1)}, bf16[4,256,256]{2,1,0:T(8,128)(2,1)}, u32[]{:S(2)}, u32[]{:S(2)}) collective-permute-start(bf16[4,256,256]{2,1,0:T(8,128)(2,1)} %get-tuple-element.52.cells), channel_id=1, source_target_pairs={{0,8},{8,0},{16,24},{24,16},{1,9},{9,1},{17,25},{25,17},{2,10},{10... | collective-permute-start | bytes 1572872 | tf_op jit(solution)/shard_map/ppermute | solution.py:819
  36.0 71.6 %collective-permute-start.3 = (bf16[12,256,256]{2,1,0:T(8,128)(2,1)}, bf16[12,256,256]{2,1,0:T(8,128)(2,1)}, u32[]{:S(2)}, u32[]{:S(2)}) collective-permute-start(bf16[12,256,256]{2,1,0:T(8,128)(2,1)} %get-tuple-element.48), channel_id=1, source_target_pairs={{0,1},{1,2},{2,3},{3,4},{4,5},{5,6},{6,7},{8,9},{9,10},{10,11},{11... | collective-permute-start | bytes 4718600 | tf_op jit(solution)/shard_map/ppermute | solution.py:820
  40.0 71.3 %collective-permute-start.4 = (bf16[12,256,256]{2,1,0:T(8,128)(2,1)}, bf16[12,256,256]{2,1,0:T(8,128)(2,1)}, u32[]{:S(2)}, u32[]{:S(2)}) collective-permute-start(bf16[12,256,256]{2,1,0:T(8,128)(2,1)} %get-tuple-element.49), channel_id=1, source_target_pairs={{1,0},{2,1},{3,2},{4,3},{5,4},{6,5},{7,6},{9,8},{10,9},{11,10},{12... | collective-permute-start | bytes 4718600 | tf_op jit(solution)/shard_map/ppermute | solution.py:821
  65.0 4.5 %collective-permute-start.9 = (bf16[8,256,256]{2,1,0:T(8,128)(2,1)}, bf16[8,256,256]{2,1,0:T(8,128)(2,1)}, u32[]{:S(2)}, u32[]{:S(2)}) collective-permute-start(bf16[8,256,256]{2,1,0:T(8,128)(2,1)} %get-tuple-element.57.row), channel_id=1, source_target_pairs={{0,8},{8,0},{16,24},{24,16},{1,9},{9,1},{17,25},{25,17},{2,10},{10... | collective-permute-start | bytes 3145736 | tf_op jit(solution)/shard_map/ppermute | solution.py:840
  65.9 16.7 %collective-permute-start.10 = (bf16[8,256,256]{2,1,0:T(8,128)(2,1)}, bf16[8,256,256]{2,1,0:T(8,128)(2,1)}, u32[]{:S(2)}, u32[]{:S(2)}) collective-permute-start(bf16[8,256,256]{2,1,0:T(8,128)(2,1)} %get-tuple-element.57.row), channel_id=1, source_target_pairs={{8,16},{16,8},{9,17},{17,9},{10,18},{18,10},{11,19},{19,11},{12,20... | collective-permute-start | bytes 3145736 | tf_op jit(solution)/shard_map/ppermute | solution.py:839
  69.4 13.2 %collective-permute-start.12 = (bf16[8,256,256]{2,1,0:T(8,128)(2,1)}, bf16[8,256,256]{2,1,0:T(8,128)(2,1)}, u32[]{:S(2)}, u32[]{:S(2)}) collective-permute-start(bf16[8,256,256]{2,1,0:T(8,128)(2,1)} %get-tuple-element.58.quads), channel_id=1, source_target_pairs={{0,8},{8,0},{16,24},{24,16},{1,9},{9,1},{17,25},{25,17},{2,10},{10... | collective-permute-start | bytes 3145736 | tf_op jit(solution)/shard_map/ppermute | solution.py:841
  114.5 21.3 %collective-permute-start.13 = (bf16[10,256,256]{2,1,0:T(8,128)(2,1)}, bf16[10,256,256]{2,1,0:T(8,128)(2,1)}, u32[]{:S(2)}, u32[]{:S(2)}) collective-permute-start(bf16[10,256,256]{2,1,0:T(8,128)(2,1)} %get-tuple-element.69), channel_id=1, source_target_pairs={{0,8},{8,16},{16,24},{1,9},{9,17},{17,25},{2,10},{10,18},{18,26},{... | collective-permute-start | bytes 3932168 | tf_op jit(solution)/shard_map/ppermute | solution.py:856
  119.7 19.2 %collective-permute-start.14 = (bf16[10,256,256]{2,1,0:T(8,128)(2,1)}, bf16[10,256,256]{2,1,0:T(8,128)(2,1)}, u32[]{:S(2)}, u32[]{:S(2)}) collective-permute-start(bf16[10,256,256]{2,1,0:T(8,128)(2,1)} %get-tuple-element.70), channel_id=1, source_target_pairs={{8,0},{16,8},{24,16},{9,1},{17,9},{25,17},{10,2},{18,10},{26,18},{... | collective-permute-start | bytes 3932168 | tf_op jit(solution)/shard_map/ppermute | solution.py:857
